TPU v7x, 128 devices: a whole 4x4x4 slice. The times are simulated.
128 devices in a mesh: dom: 8 (over y, core), cls: 16 (over x, z).
Axes of the slice: x: 4, y: 4, z: 4, core: 2. Of those that a mesh axis runs over, the one named last changes fastest.
Arguments:
- particles: bfloat16 [6144, 64, 288], P(('dom', 'cls')), may hold values from -6 to 6
- references: bfloat16 [400, 64, 288], P('cls'), may hold values from -6 to 6
- class_block: int32 [6144, 1], P(('dom', 'cls')), may hold values from 0 to 15; in each aligned block of 48 rows (0 to 47, 48 to 95, ...) at most 6 rows name the same one
- class_local: int32 [6144], P(('dom', 'cls')), may hold values from 0 to 24
- rotation: int32 [6144], P(('dom', 'cls')), may hold values from 0 to 35
- shifts: int32 [6144, 2], P(('dom', 'cls')), may hold values from -5 to 5
- defocus: int32 [6144], P(('dom', 'cls')), may hold values from 0 to 15
Outputs:
- best_score: float32 [6144], P(('dom', 'cls'))
- class_average: float32 [400, 64, 288], P('cls', 'dom')
Inputs may be any that keep to these rules, and one draw needn't show every extreme that they name: `class_block`: in the rows of one device no class block is named more than 6 times, and some class block is named exactly 6 times by some device.
All inputs are finite; a program needn't handle non-finite values.
Results may differ from a plain program's by a relative error of at most 0.0045.
Values may be sent and summed in bfloat16 or wider, within the bound.
No kernel may reach another device: no remote copies, remote signals or barrier semaphores. Data moves between devices by JAX's collectives and lax.ppermute only.
A program may use at most 128 MiB of HBM per device.

v0:
```python
import functools
import math

import jax
import jax.numpy as jnp
import ml_dtypes
import numpy as np
from jax import lax
from jax.experimental import pallas as pl
from jax.experimental.pallas import tpu as pltpu
from jax.sharding import PartitionSpec as P

ROT = 36
BOX = 128
NBINS = 16
EPSILON = 1e-06
CYC = 64
ANG = 144
ROW = 2 * ANG
SHIFT = 5
PD = 48
KD = 25
OWN = 16
DOM = 8
BAND = CYC // DOM
UNITS = 18
HALF = UNITS // 2
MH = HALF * 8
HEAD = 192
NORM0 = 96
HROWS = HEAD + MH * 24
HH = 40
MP = 2 * HH
CHUNKS = 19
UROWS = CHUNKS * PD
SROWS = 480
KPAD = 512
STEP = 16
F32 = jnp.float32
BF16 = jnp.bfloat16
VMEM_BYTES = 58 * 1024 * 1024
NT = (((1,), (1,)), ((), ()))


def unit_harmonics():
    rows = []
    for unit in range(UNITS):
        plus, minus = (0, 18) if unit == 0 else (unit, ROT - unit)
        rows.append([plus + ROT * q for q in range(4)] + [minus + ROT * q for q in range(4)])
    return np.array(rows).reshape(2, MH)


def dft_rows():
    turn = np.arange(ANG)[:, None] * np.arange(ANG)[None, :] % ANG
    angle = turn.astype(np.float32) * np.float32(2.0 * math.pi / ANG)
    cosine = np.cos(angle.astype(np.float64))
    sine = np.sin(angle.astype(np.float64))
    upper = np.concatenate([cosine, -sine], axis=1)
    lower = np.concatenate([sine, cosine], axis=1)
    full = np.concatenate([upper, lower], axis=0).astype(np.float32).astype(ml_dtypes.bfloat16)
    halves = unit_harmonics()
    split = []
    for core in range(2):
        mine, other = halves[core], halves[1 - core]
        rows = np.zeros((4 * MP, ROW), ml_dtypes.bfloat16)
        for index, columns in enumerate((mine, ANG + mine, other, ANG + other)):
            for parity in range(2):
                start = index * MP + parity * HH
                rows[start : start + MH // 2] = full[:, columns[parity::2]].T
        split.append(rows)
    return full, np.stack(split)


def wide_columns(full):
    order = np.concatenate([np.arange(256)] + [np.arange(256, 288)] * 4)
    swapped = np.concatenate([-full[:, ANG:], full[:, :ANG]], axis=1)
    return np.concatenate([full[:, order], swapped[:, order]], axis=1), order


def turn_rows(order):
    harmonic = order % ANG
    turn = np.arange(ROT)[:, None] * 4 * harmonic[None, :] % ANG
    angle = turn * (2.0 * math.pi / ANG)
    angle = angle.reshape(ROT, 3, 128)
    rest = np.zeros((ROT, 2, 128))
    return np.concatenate([np.cos(angle), np.sin(angle), rest], axis=1).astype(np.float32)


def ctf_values():
    radius = (np.arange(CYC) + 1) / CYC
    level = np.arange(NBINS) / NBINS
    phase = math.pi * (3.0 + 9.0 * level[:, None]) * (radius * radius)[None, :]
    return 0.995 * np.sin(phase) + 0.1 * np.cos(phase)


def shift_rows():
    angle = np.arange(ANG) * (2.0 * math.pi / ANG)
    scale = 2.0 * math.pi / BOX * np.concatenate([np.arange(8), 8 * np.arange(8)])
    size = np.arange(SHIFT + 1)
    out = []
    for beam in (np.cos(angle), np.sin(angle)):
        phase = size[:, None, None] * scale[None, :, None] * beam[None, None, :]
        phase = np.concatenate([phase, phase], axis=2)
        out += [np.cos(phase), np.sin(phase)]
    return np.stack(out).astype(np.float32)


def swap_matrix():
    swap = np.zeros((ROW, ROW), np.float32)
    index = np.arange(ANG)
    swap[ANG + index, index] = -1.0
    swap[index, ANG + index] = 1.0
    return swap.astype(ml_dtypes.bfloat16)


def pair_signs():
    signs = np.zeros((2, 3, MH, 128), np.float32)
    for core in range(2):
        for row in range(MH):
            unit, place = core * HALF + row // 8, row % 8
            if unit == 0:
                signs[core, 0 if place < 4 else 1, row] = 1.0
            else:
                signs[core, 0, row] = 1.0
                flip = 1.0 if place < 4 else -1.0
                signs[core, 2, row, :64] = -flip
                signs[core, 2, row, 64:] = flip
    signs = np.pad(signs.transpose(0, 2, 1, 3), ((0, 0), (0, 0), (0, 5), (0, 0)))
    return signs


def whole(shape):
    return pl.BlockSpec(shape, lambda *_: (0,) * len(shape))


def merge_halves(real, imag, low):
    first = jnp.where(low, real, pltpu.roll(imag, 64, 1))
    second = jnp.where(low, pltpu.roll(real, 64, 1), imag)
    return first, second


def harmonics_kernel(
    core, refs_any, table_any, squares_any, out, refs, table, squares, scratch, energy, norms, sems
):
    copies = [pltpu.make_async_copy(table_any.at[core[0]], table, sems.at[0])]
    for index in range(4):
        chunk = pl.ds(index * 512, 512 if index < 3 else 64)
        copies.append(
            pltpu.make_async_copy(refs_any.at[chunk, :], refs.at[chunk, :], sems.at[index + 1])
        )
    copies.append(pltpu.make_async_copy(squares_any, squares, sems.at[5]))
    for copy in copies:
        copy.start()
    scratch[0:HEAD, :] = jnp.zeros((HEAD, 128), F32)
    energy[...] = jnp.zeros_like(energy)
    low = lax.broadcasted_iota(jnp.int32, (MP, 128), 1) < 64
    copies[0].wait()
    rows = table[...]

    def place(klass, value):
        if klass == 24:
            scratch[0:MP, :] = value
            return
        for parity in range(2):
            start = HEAD + (parity * 16 + klass if klass < 16 else 16 + parity * 8 + klass)
            piece = value[parity * HH : parity * HH + MH // 2]
            scratch[pl.ds(start, MH // 2, stride=48), :] = piece

    for group in range(7):
        start, width = (group * 256, 256) if group < 6 else (KD * CYC - 128, 128)
        if group % 2 == 0:
            copies[1 + group // 2].wait()
        full = lax.dot_general(rows, refs[start : start + width, :], NT, preferred_element_type=F32)
        kept = full.astype(BF16).astype(F32)
        total = jnp.sum(kept * kept, axis=0, keepdims=True)
        if group < 6:
            energy[group : group + 1, :] = total
        else:
            energy[group : group + 1, 0:128] = jnp.where(low[0:1], pltpu.roll(total, 64, 1), 0.0)
        for pair in range(width // 128):
            lanes = slice(pair * 128, pair * 128 + 128)
            first, second = merge_halves(full[0:MP, lanes], full[MP : 2 * MP, lanes], low)
            if group < 6:
                place(group * 4 + pair * 2, first)
                place(group * 4 + pair * 2 + 1, second)
            else:
                place(24, second)
    copies[5].wait()
    for sub in range(4):
        lanes = slice(sub // 2 * 128, sub // 2 * 128 + 128)
        power = jnp.dot(
            energy[:, lanes],
            squares[sub % 2],
            precision=lax.Precision.HIGHEST,
            preferred_element_type=F32,
        )
        norms[pl.ds(sub, 8, stride=4), :] = power
    scale = (1.0 / ANG) / jnp.sqrt(norms[...] * (1.0 / ANG) + EPSILON)
    scale = jnp.where(lax.broadcasted_iota(jnp.int32, (32, 128), 1) < NBINS, scale, 0.0)
    high = scale.astype(BF16).astype(F32)
    scratch[NORM0 : NORM0 + 32, :] = high + pltpu.roll(scale - high, NBINS, 1)
    out[...] = scratch[...].astype(BF16)


def own_harmonics(core, references, table):
    squares = np.zeros((2, 128, 128), np.float32)
    ctf = ctf_values()
    for sub in range(2):
        squares[sub, 64 * sub : 64 * sub + 64, :NBINS] = (ctf * ctf).T
    return pl.pallas_call(
        harmonics_kernel,
        in_specs=[
            pl.BlockSpec(memory_space=pltpu.SMEM),
            pl.BlockSpec(memory_space=pl.ANY),
            pl.BlockSpec(memory_space=pl.ANY),
            pl.BlockSpec(memory_space=pl.ANY),
        ],
        out_specs=pl.BlockSpec(memory_space=pltpu.VMEM),
        scratch_shapes=[
            pltpu.VMEM((KD * CYC, ROW), BF16),
            pltpu.VMEM((4 * MP, ROW), BF16),
            pltpu.VMEM((2, 128, 128), F32),
            pltpu.VMEM((HROWS, 128), F32),
            pltpu.VMEM((8, 256), F32),
            pltpu.VMEM((32, 128), F32),
            pltpu.SemaphoreType.DMA((6,)),
        ],
        out_shape=jax.ShapeDtypeStruct((HROWS, 128), BF16),
        compiler_params=pltpu.CompilerParams(vmem_limit_bytes=VMEM_BYTES),
        cost_estimate=pl.CostEstimate(
            flops=4000000000, bytes_accessed=12000000, transcendentals=0
        ),
        name="harmonics",
    )(core, references.reshape(KD * CYC, ROW), table, jnp.asarray(squares))


def shift_group(scalars, first, data, swap, phases):
    crossed = jnp.dot(data, swap, preferred_element_type=F32)
    shifted = []
    for sub in range(4):
        move_x = scalars[0, first + sub]
        move_y = scalars[1, first + sub]
        sign_x = jnp.where(move_x < 0, -1.0, 1.0)
        sign_y = jnp.where(move_y < 0, -1.0, 1.0)
        size_x = jnp.abs(move_x)
        size_y = jnp.abs(move_y)
        cos_x = phases[0, size_x]
        sin_x = phases[1, size_x] * sign_x
        cos_y = phases[2, size_y]
        sin_y = phases[3, size_y] * sign_y
        cosine = cos_x * cos_y - sin_x * sin_y
        sine = sin_x * cos_y + cos_x * sin_y
        near_cos, near_sin = cosine[0:8], sine[0:8]
        for jump in range(8):
            far_cos = cosine[8 + jump : 9 + jump]
            far_sin = sine[8 + jump : 9 + jump]
            rows = slice(sub * CYC + jump * 8, sub * CYC + jump * 8 + 8)
            value = data[rows].astype(F32) * (near_cos * far_cos - near_sin * far_sin)
            value = value + crossed[rows] * (near_sin * far_cos + near_cos * far_sin)
            shifted.append(value)
    return jnp.concatenate(shifted, axis=0).astype(BF16)


def spread_kernel(scalars, parts, wide, swap, phases, turn, ctf_columns, spread, turned, tails):
    step = pl.program_id(0)
    lane = lax.broadcasted_iota(jnp.int32, (1, 128), 1)
    group = lax.broadcasted_iota(jnp.int32, (16, 128), 1) // 32

    def one_group(quad, carry):
        first = step * STEP + quad * 4
        start = pl.multiple_of(quad * 256, 256)
        data = parts[pl.ds(start, 256), :]
        shifted = shift_group(scalars, first, data, swap[...], phases)
        natural = jnp.dot(shifted, wide[...], preferred_element_type=F32)
        for sub in range(4):
            index = first + sub
            rows = slice(sub * CYC, sub * CYC + CYC)
            angles = turn[scalars[3, index]]
            chosen = jnp.where(lane == scalars[2, index], ctf_columns[...], 0.0)
            contrast = jnp.sum(chosen, axis=1, keepdims=True)
            for tile in range(3):
                lanes = slice(tile * 128, tile * 128 + 128)
                cos_rot = angles[tile : tile + 1, :]
                sin_rot = angles[tile + 3 : tile + 4, :]
                there = slice(384 + tile * 128, 384 + tile * 128 + 128)
                value = natural[rows, lanes] * cos_rot + natural[rows, there] * sin_rot
                value = contrast * value
                if tile < 2:
                    for band in range(DOM):
                        begin = band * UROWS + tile * PD + index
                        piece = value[band * BAND : band * BAND + BAND]
                        turned[pl.ds(begin, BAND, stride=2 * PD), :] = piece
                else:
                    tails[sub] = value
                    packed = tails[sub, pl.ds(0, 16, stride=4), :]
                    for place in range(1, 4):
                        other = tails[sub, pl.ds(place, 16, stride=4), :]
                        packed = jnp.where(group == place, other, packed)
                    tails[sub, 0:16, :] = packed
                    for half in range(2):
                        piece = tails[sub, pl.ds(half, DOM, stride=2), :]
                        turned[pl.ds((16 + half) * PD + index, DOM, stride=UROWS), :] = piece
            label = jnp.where(lane == scalars[2, index], 1.0, 0.0)
            label = jnp.where(lane == 16, scalars[4, index].astype(F32), label)
            label = jnp.where(lane == 17, scalars[5, index].astype(F32), label)
            label = jnp.broadcast_to(label, (DOM, 128))
            turned[pl.ds(18 * PD + index, DOM, stride=UROWS), :] = label
        return carry

    lax.fori_loop(0, STEP // 4, one_group, 0, unroll=True)

    @pl.when(step == PD // STEP - 1)
    def _():
        spread[...] = turned[...].astype(BF16)


def spread_bands(particles, scalars, full_table):
    wide, order = wide_columns(full_table)
    ctf_columns = np.zeros((CYC, 128), np.float32)
    ctf_columns[:, :NBINS] = ctf_values().T
    return pl.pallas_call(
        spread_kernel,
        grid_spec=pltpu.PrefetchScalarGridSpec(
            num_scalar_prefetch=1,
            grid=(PD // STEP,),
            in_specs=[
                pl.BlockSpec((STEP * CYC, ROW), lambda i, sc: (i, 0)),
                whole((ROW, 768)),
                whole((ROW, ROW)),
                whole((4, SHIFT + 1, 16, ROW)),
                whole((ROT, 8, 128)),
                whole((CYC, 128)),
            ],
            out_specs=whole((DOM * UROWS, 128)),
            scratch_shapes=[
                pltpu.VMEM((DOM * UROWS, 128), F32),
                pltpu.VMEM((4, CYC, 128), F32),
            ],
        ),
        out_shape=jax.ShapeDtypeStruct((DOM * UROWS, 128), BF16),
        compiler_params=pltpu.CompilerParams(vmem_limit_bytes=VMEM_BYTES // 2),
        cost_estimate=pl.CostEstimate(
            flops=9000000000, bytes_accessed=27000000, transcendentals=0
        ),
        name="spread",
    )(
        scalars,
        particles,
        jnp.asarray(wide),
        jnp.asarray(swap_matrix()),
        jnp.asarray(shift_rows()),
        jnp.asarray(turn_rows(order)),
        jnp.asarray(ctf_columns),
    )


def weight_kernel(core, scalars, parts, table, swap, phases, ctf_rows, mine, other, weighted):
    step = pl.program_id(0)
    low = lax.broadcasted_iota(jnp.int32, (MP, 128), 1) < 64

    def one_group(quad, carry):
        first = step * STEP + quad * 4
        start = pl.multiple_of(quad * 256, 256)
        data = parts[pl.ds(start, 256), :]
        shifted = shift_group(scalars, first, data, swap[...], phases)
        full = lax.dot_general(table[0], shifted, NT, preferred_element_type=F32)
        for pair in range(2):
            lanes = slice(pair * 128, pair * 128 + 128)
            for side in range(2):
                base = side * 2 * MP
                both = merge_halves(
                    full[base : base + MP, lanes], full[base + MP : base + 2 * MP, lanes], low
                )
                for which in range(2):
                    index = first + pair * 2 + which
                    contrast = ctf_rows[pl.ds(scalars[2, index], 1), :]
                    value = both[which] * contrast
                    for parity in range(2):
                        begin = (side * MH + parity) * PD + index
                        piece = value[parity * HH : parity * HH + MH // 2]
                        weighted[pl.ds(begin, MH // 2, stride=2 * PD), :] = piece
        return carry

    lax.fori_loop(0, STEP // 4, one_group, 0, unroll=True)

    @pl.when(step == PD // STEP - 1)
    def _():
        mine[...] = weighted[0 : MH * PD, :].astype(BF16)
        other[...] = weighted[MH * PD :, :].astype(BF16)


def weighted_spectra(core, particles, scalars, table):
    ctf = ctf_values().astype(np.float32)
    half_shape = jax.ShapeDtypeStruct((MH * PD, 128), BF16)
    return pl.pallas_call(
        weight_kernel,
        grid_spec=pltpu.PrefetchScalarGridSpec(
            num_scalar_prefetch=2,
            grid=(PD // STEP,),
            in_specs=[
                pl.BlockSpec((STEP * CYC, ROW), lambda i, core, sc: (i, 0)),
                pl.BlockSpec((1, 4 * MP, ROW), lambda i, core, sc: (core[0], 0, 0)),
                whole((ROW, ROW)),
                whole((4, SHIFT + 1, 16, ROW)),
                whole((NBINS, 128)),
            ],
            out_specs=[whole((MH * PD, 128)), whole((MH * PD, 128))],
            scratch_shapes=[pltpu.VMEM((2 * MH * PD, 128), F32)],
        ),
        out_shape=[half_shape, half_shape],
        compiler_params=pltpu.CompilerParams(vmem_limit_bytes=VMEM_BYTES // 2),
        cost_estimate=pl.CostEstimate(
            flops=10000000000, bytes_accessed=30000000, transcendentals=0
        ),
        name="weights",
    )(
        core,
        scalars,
        particles,
        table,
        jnp.asarray(swap_matrix()),
        jnp.asarray(shift_rows()),
        jnp.asarray(np.concatenate([ctf, ctf], axis=1)),
    )


def fold_kernel(layout, count, core, *refs):
    pieces = refs[:count]
    own, far, signs, bins, kept_out, sent_out, norm = refs[count : count + 7]
    kept, sent, blocks, held, last, scale_rows, arrivals, leaving = refs[count + 7 :]
    copies = []
    for index, (slot, start, rows, first) in enumerate(layout):
        source = pieces[index].at[pl.ds(first, rows), :]
        target = blocks.at[slot, pl.ds(start, rows), :]
        copies.append(pltpu.make_async_copy(source, target, arrivals.at[index]))
    for copy in copies:
        copy.start()
    held[OWN * KD :, :] = jnp.zeros((KPAD - OWN * KD, 1024), BF16)
    scale_rows[...] = jnp.zeros_like(scale_rows)
    lane = lax.broadcasted_iota(jnp.int32, (PD, 128), 1)
    row = lax.broadcasted_iota(jnp.int32, (PD, 128), 0)
    level = jnp.zeros((PD, 128), jnp.int32)
    for index in range(PD):
        level = jnp.where(row == index, bins[index], level)
    hits = jnp.where((lane == level) | (lane == level + NBINS), 1.0, 0.0).astype(BF16)

    def outgoing(unit):
        both = pl.ds(2 * unit, 2)
        return (
            pltpu.make_async_copy(sent.at[both], sent_out.at[both], leaving.at[unit, 0]),
            pltpu.make_async_copy(kept.at[both], kept_out.at[both], leaving.at[unit, 1]),
        )

    def one_unit(unit, carry):
        parts_a, parts_b = [], []
        for place in range(8):
            harmonic = unit * 8 + place
            row = jnp.concatenate([own[harmonic], far[harmonic]], axis=0).astype(F32)
            factor = signs[core[0], harmonic]
            parts_a.append((row * factor[0:1]).astype(BF16))
            swapped = pltpu.roll(row, 64, 1) * factor[2:3]
            parts_b.append((row * factor[1:2] + swapped).astype(BF16))
        left = jnp.concatenate(
            [jnp.concatenate(parts_a, axis=1), jnp.concatenate(parts_b, axis=1)], axis=0
        )
        for pair in range(4):
            start = pl.multiple_of(HEAD + unit * 192 + pair * 48, 16)
            for parity in range(2):
                place = pair * 2 + parity
                lanes = slice(place * 128, place * 128 + 128)
                for slot in range(OWN):
                    held[slot * 16 : slot * 16 + 16, lanes] = blocks[
                        slot, pl.ds(start + parity * 16, 16), :
                    ]
                begin = pl.multiple_of((parity * HH + unit * 4 + pair) * OWN, OWN)
                held[OWN * 24 : OWN * KD, lanes] = last[pl.ds(begin, OWN), :].astype(BF16)
            for slot in range(0, OWN, 2):
                one = blocks[slot, pl.ds(start + 32, 16), :].astype(F32)
                two = blocks[slot + 1, pl.ds(start + 32, 16), :].astype(F32)
                for parity in range(2):
                    place = pair * 2 + parity
                    lanes = slice(place * 128, place * 128 + 128)
                    rows = slice(parity * 8, parity * 8 + 8)
                    both = jnp.concatenate([one[rows], two[rows]], axis=0).astype(BF16)
                    held[256 + slot * 8 : 256 + slot * 8 + 16, lanes] = both
        folded = lax.dot_general(left, held[...], NT, preferred_element_type=F32).astype(BF16)
        kept[2 * unit] = folded[0:PD]
        sent[2 * unit] = folded[PD : 2 * PD]
        kept[2 * unit + 1] = folded[2 * PD : 3 * PD]
        sent[2 * unit + 1] = folded[3 * PD : 4 * PD]
        for copy in outgoing(unit):
            copy.start()
        return carry

    for copy, (slot, start, rows, first) in zip(copies, layout):
        if start < HROWS // 2:
            copy.wait()
    for slot in range(OWN):
        last[pl.ds(slot, MP, stride=OWN), :] = blocks[slot, 0:MP, :].astype(F32)
        scales = blocks[slot, NORM0 : NORM0 + 32, :].astype(F32)
        scale_rows[slot * 16 : slot * 16 + 16, :] = scales[0:16]
        scale_rows[256 + slot * 8 : 256 + slot * 8 + 8, :] = scales[16:24]
        scale_rows[OWN * 24 + slot : OWN * 24 + slot + 1, :] = scales[24:25]
    table = scale_rows[...].astype(BF16)
    norm[...] = lax.dot_general(hits, table, NT, preferred_element_type=F32)
    lax.fori_loop(0, 4, one_unit, 0, unroll=True)
    for copy, (slot, start, rows, first) in zip(copies, layout):
        if start >= HROWS // 2:
            copy.wait()
    lax.fori_loop(4, HALF, one_unit, 0, unroll=True)
    for unit in range(HALF):
        for copy in outgoing(unit):
            copy.wait()


def fold(core, arrived, own, far, bins):
    layout = tuple((slot, start, rows, first) for slot, start, rows, first, _ in arrived)
    count = len(layout)
    piece = jax.ShapeDtypeStruct((UNITS, PD, KPAD), BF16)
    vmem = pl.BlockSpec(memory_space=pltpu.VMEM)
    return pl.pallas_call(
        functools.partial(fold_kernel, layout, count),
        in_specs=[pl.BlockSpec(memory_space=pltpu.SMEM)]
        + [pl.BlockSpec(memory_space=pl.ANY)] * count
        + [vmem] * 3
        + [pl.BlockSpec(memory_space=pltpu.SMEM)],
        out_specs=[pl.BlockSpec(memory_space=pl.ANY)] * 2 + [vmem],
        scratch_shapes=[
            pltpu.VMEM((UNITS, PD, KPAD), BF16),
            pltpu.VMEM((UNITS, PD, KPAD), BF16),
            pltpu.VMEM((OWN, HROWS, 128), BF16),
            pltpu.VMEM((KPAD, 1024), BF16),
            pltpu.VMEM((MP * OWN, 128), F32),
            pltpu.VMEM((KPAD, 128), F32),
            pltpu.SemaphoreType.DMA((count,)),
            pltpu.SemaphoreType.DMA((HALF, 2)),
        ],
        out_shape=[piece, piece, jax.ShapeDtypeStruct((PD, KPAD), F32)],
        compiler_params=pltpu.CompilerParams(vmem_limit_bytes=VMEM_BYTES),
        cost_estimate=pl.CostEstimate(
            flops=9000000000, bytes_accessed=27000000, transcendentals=0
        ),
        name="fold",
    )(
        core,
        *[value for *_, value in arrived],
        own.reshape(MH, PD, 128),
        far.reshape(MH, PD, 128),
        jnp.asarray(pair_signs()),
        bins,
    )


def moved_by(value, along_x, along_z):
    moves = [
        (x * 4 + z, (x + along_x) % 4 * 4 + (z + along_z) % 4) for x in range(4) for z in range(4)
    ]
    return lax.ppermute(value, "cls", moves)


def join_kernel(left, right, two_x, down, up, two_z, low, high, held, sems):
    half = HROWS // 2
    inward, outward = [], []
    for index, source in enumerate((left, right, two_x, down, up, two_z)):
        first = 0 if index < 3 else half
        target = (low if index < 3 else high).at[pl.ds(index % 3 * half, half), :]
        inward.append(
            pltpu.make_async_copy(source.at[pl.ds(first, half), :], held.at[index], sems.at[index])
        )
        outward.append(pltpu.make_async_copy(held.at[index], target, sems.at[6 + index]))
    for copy in inward:
        copy.start()
    for come, go in zip(inward, outward):
        come.wait()
        go.start()
    for copy in outward:
        copy.wait()


def join(*blocks):
    anywhere = pl.BlockSpec(memory_space=pl.ANY)
    rows = jax.ShapeDtypeStruct((3 * HROWS // 2, 128), BF16)
    return pl.pallas_call(
        join_kernel,
        in_specs=[anywhere] * 6,
        out_specs=[anywhere] * 2,
        scratch_shapes=[
            pltpu.VMEM((6, HROWS // 2, 128), BF16),
            pltpu.SemaphoreType.DMA((12,)),
        ],
        out_shape=[rows, rows],
        compiler_params=pltpu.CompilerParams(vmem_limit_bytes=VMEM_BYTES),
        cost_estimate=pl.CostEstimate(
            flops=2000000000, bytes_accessed=6000000, transcendentals=0
        ),
        name="join",
    )(*blocks)


def cut_kernel(low_before, low_after, high_before, high_after, *refs):
    outs, held, sems = refs[:4], refs[4], refs[5]
    part = 3 * HROWS // 4
    inward, outward = [], []
    for index, source in enumerate((low_before, low_after, high_before, high_after)):
        chunk = pl.ds(index % 2 * part, part)
        inward.append(pltpu.make_async_copy(source.at[chunk, :], held.at[index], sems.at[index]))
        outward.append(pltpu.make_async_copy(held.at[index], outs[index], sems.at[4 + index]))
    for copy in inward:
        copy.start()
    for come, go in zip(inward, outward):
        come.wait()
        go.start()
    for copy in outward:
        copy.wait()


def cut(*rows):
    anywhere = pl.BlockSpec(memory_space=pl.ANY)
    part = jax.ShapeDtypeStruct((3 * HROWS // 4, 128), BF16)
    return pl.pallas_call(
        cut_kernel,
        in_specs=[anywhere] * 4,
        out_specs=[anywhere] * 4,
        scratch_shapes=[
            pltpu.VMEM((4, 3 * HROWS // 4, 128), BF16),
            pltpu.SemaphoreType.DMA((8,)),
        ],
        out_shape=[part] * 4,
        compiler_params=pltpu.CompilerParams(vmem_limit_bytes=VMEM_BYTES),
        cost_estimate=pl.CostEstimate(
            flops=2000000000, bytes_accessed=6000000, transcendentals=0
        ),
        name="cut",
    )(*rows)


def gather_blocks(block, spread_of):
    half, part = HROWS // 2, 3 * HROWS // 4
    steps = (-1, 1, 2)
    by_x = [moved_by(block, -step, 0) for step in steps]
    by_z = [moved_by(block, 0, -step) for step in steps]
    by_x[2], spread = spread_of(by_x[2])
    low_rows, high_rows = join(*by_x, *by_z)
    low_far = [moved_by(low_rows, 0, 1), moved_by(low_rows, 0, -1)]
    high_far = [moved_by(high_rows, 1, 0), moved_by(high_rows, -1, 0)]
    arrived = lax.all_to_all(spread.reshape(DOM, UROWS, 128), "dom", 0, 0, tiled=True)
    sums = class_sums(arrived)
    low_far, high_far, sums = lax.optimization_barrier((low_far, high_far, sums))
    parts = cut(*low_far, *high_far)
    low_two = moved_by(parts[0], 0, 1), moved_by(parts[1], 0, -1)
    high_two = moved_by(parts[2], 1, 0), moved_by(parts[3], -1, 0)

    def slot(x, z):
        return x % 4 * 4 + z % 4

    pieces = []
    for start in (0, half):
        pieces.append((slot(0, 0), start, half, start, block))
        pieces += [(slot(step, 0), start, half, start, by_x[i]) for i, step in enumerate(steps)]
        pieces += [(slot(0, step), start, half, start, by_z[i]) for i, step in enumerate(steps)]
        near, two = (low_far, low_two) if start == 0 else (high_far, high_two)
        for j, inner in enumerate(steps):
            for i, outer in enumerate(steps[:2]):
                place = slot(inner, outer) if start == 0 else slot(outer, inner)
                pieces.append((place, start, half, j * half, near[i]))
            place = slot(inner, 2) if start == 0 else slot(2, inner)
            for i in range(2):
                first = max(j * half, i * part)
                last = min(j * half + half, i * part + part)
                if first < last:
                    begin = start + first - j * half
                    pieces.append((place, begin, last - first, first - i * part, two[i]))
    return pieces, low_rows, sums


def weigh(total, coefficient, value):
    if abs(coefficient) < 1e-12:
        return total
    if abs(coefficient - 1.0) < 1e-12:
        return value if total is None else total + value
    if abs(coefficient + 1.0) < 1e-12:
        return -value if total is None else total - value
    term = value * coefficient
    return term if total is None else total + term


def best_rotation(cosines, sines):
    best = None
    for parity in range(2):
        sign = 1.0 if parity == 0 else -1.0
        even = {0: cosines[0] + sign * cosines[18]}
        odd = {}
        for unit in range(1, 9):
            even[unit] = cosines[unit] + sign * cosines[18 - unit]
            odd[unit] = sines[unit] - sign * sines[18 - unit]
        even[9] = cosines[9]
        odd[9] = sines[9]
        for rotation in range(parity, 10, 2):
            sums = {}
            for name, values, wave in (("e", even, math.cos), ("o", odd, math.sin)):
                for rest in range(2):
                    total = None
                    for unit, value in values.items():
                        if unit % 2 == rest:
                            angle = math.pi * ((unit * rotation) % 36) / 18.0
                            total = weigh(total, wave(angle), value)
                    sums[name, rest] = total

            def joined(first, second, flip):
                if first is None and second is None:
                    return None
                if second is None:
                    return first
                if first is None:
                    return second
                return first - second if flip else first + second

            for flip in (False, True) if rotation < 9 else (False,):
                value = joined(sums["e", 0], sums["e", 1], flip)
                swing = joined(sums["o", 1], sums["o", 0], flip)
                if swing is not None:
                    value = value + jnp.abs(swing)
                best = value if best is None else jnp.maximum(best, value)
    return best


def score_kernel(core, kept, came, norm, out, found):
    step = pl.program_id(0)

    def score(low, high):
        for block in range(2):
            rows = slice(block * 8, block * 8 + 8)
            every = slice(0, 16)
            best = None
            for tile in range(KPAD // 128):
                lanes = slice(tile * 128, tile * 128 + 128)
                cosines, sines = {}, {}
                for unit in range(UNITS):
                    source = low if unit < HALF else high
                    place = unit % HALF * 2
                    cosines[unit] = source[place, every, lanes].astype(F32)[rows]
                    sines[unit] = source[place + 1, every, lanes].astype(F32)[rows]
                cosines[18] = sines[0]
                value = best_rotation(cosines, sines) * norm[rows, lanes]
                if tile == 3:
                    lane = lax.broadcasted_iota(jnp.int32, (8, 128), 1)
                    value = jnp.where(lane < OWN * KD - 384, value, -3e38)
                best = value if best is None else jnp.maximum(best, value)
            best = jnp.broadcast_to(jnp.max(best, axis=1, keepdims=True), (8, 128))
            found[pl.ds(pl.multiple_of(step * 16 + block * 8, 8), 8), :] = best

    @pl.when(core[0] == 0)
    def _():
        score(kept, came)

    @pl.when(core[0] == 1)
    def _():
        score(came, kept)

    @pl.when(step == PD // 16 - 1)
    def _():
        out[...] = found[...].T[0:1, 0:PD]


def scores(core, kept, came, norm):
    return pl.pallas_call(
        score_kernel,
        grid_spec=pltpu.PrefetchScalarGridSpec(
            num_scalar_prefetch=1,
            grid=(PD // 16,),
            in_specs=[
                pl.BlockSpec((UNITS, 16, KPAD), lambda i, core: (0, i, 0)),
                pl.BlockSpec((UNITS, 16, KPAD), lambda i, core: (0, i, 0)),
                pl.BlockSpec((16, KPAD), lambda i, core: (i, 0)),
            ],
            out_specs=whole((1, PD)),
            scratch_shapes=[pltpu.VMEM((PD, 128), F32)],
        ),
        out_shape=jax.ShapeDtypeStruct((1, PD), F32),
        compiler_params=pltpu.CompilerParams(vmem_limit_bytes=VMEM_BYTES),
        cost_estimate=pl.CostEstimate(
            flops=3000000000, bytes_accessed=9000000, transcendentals=0
        ),
        name="scores",
    )(core, kept, came, norm)


def class_sum_kernel(arrived, out, last):
    labels = arrived[:, 18 * PD : 19 * PD, :].astype(F32).reshape(DOM * PD, 128)
    block = labels[:, 16:17]
    local = labels[:, 17:18]
    row = jnp.where(local < 23.5, block * 24.0 + local, block + 384.0)
    lane = lax.broadcasted_iota(jnp.int32, (DOM * PD, KPAD), 1).astype(F32)
    hits = jnp.where(lane == row, 1.0, 0.0).T[0 : OWN * KD].astype(BF16)
    last[...] = jnp.zeros_like(last)
    for pair in range(10):
        pieces = [2 * pair, 2 * pair + 1] if pair < 9 else [18]
        right = jnp.concatenate(
            [arrived[:, c * PD : c * PD + PD, :].reshape(DOM * PD, 128) for c in pieces], axis=1
        )
        total = jnp.dot(hits, right, preferred_element_type=F32)
        sums = [total[:, i * 128 : i * 128 + 128] for i in range(len(pieces))]
        for place, value in zip(pieces, sums):
            last[pl.ds(24 + place, OWN, stride=48), :] = value[OWN * 24 :]
        if pair < 9:
            both = jnp.concatenate(
                [value[0 : OWN * 24].reshape(OWN, 24, 128) for value in sums], axis=1
            )
            out[:, pair * 48 : pair * 48 + 48, :] = both.astype(BF16)
        else:
            for owner in range(OWN):
                last[owner * 48 : owner * 48 + 24, :] = sums[0][owner * 24 : owner * 24 + 24]
    out[:, 432:480, :] = last[...].reshape(OWN, 48, 128).astype(BF16)


def class_sums(arrived):
    return pl.pallas_call(
        class_sum_kernel,
        in_specs=[pl.BlockSpec(memory_space=pltpu.VMEM)],
        out_specs=pl.BlockSpec(memory_space=pltpu.VMEM),
        scratch_shapes=[pltpu.VMEM((OWN * 48, 128), F32)],
        out_shape=jax.ShapeDtypeStruct((OWN, SROWS, 128), BF16),
        compiler_params=pltpu.CompilerParams(vmem_limit_bytes=VMEM_BYTES // 2),
        cost_estimate=pl.CostEstimate(
            flops=3000000000, bytes_accessed=9000000, transcendentals=0
        ),
        name="class_sums",
    )(arrived)


def average_kernel(dom, arrived, squares, out, left, middle, right):
    total = arrived[0].astype(F32)
    for source in range(1, OWN):
        total = total + arrived[source].astype(F32)
    counts = jnp.concatenate([total[432:456], total[472:480]], axis=0)
    below = jnp.dot(counts, squares[0], precision=lax.Precision.HIGHEST, preferred_element_type=F32)
    below = below + 1.0
    for cycle in range(BAND):
        usual = below[0:24, cycle : cycle + 1]
        final = below[26:27, cycle : cycle + 1]
        for tile, target in ((0, left), (1, middle), (2, right)):
            if tile < 2:
                piece, turn = cycle * 2 + tile, 0
            else:
                piece, turn = 16 + cycle // 4, (128 - cycle % 4 * 32) % 128
            value = total[piece * 24 : piece * 24 + 24] / usual
            end = total[456 + piece : 457 + piece] / final
            if turn:
                value = pltpu.roll(value, turn, 1)
                end = pltpu.roll(end, turn, 1)
            target[pl.ds(cycle, 24, stride=BAND), :] = value
            target[24 * BAND + cycle : 24 * BAND + cycle + 1, :] = end
    out[:, 0:128] = left[...]
    out[:, 128:256] = middle[...]
    out[:, 256:288] = right[:, 0:32]


def averages(dom, arrived):
    ctf = ctf_values()
    squares = np.zeros((DOM, 128, 128), np.float32)
    for band in range(DOM):
        squares[band, :NBINS, :BAND] = (ctf * ctf)[:, band * BAND : band * BAND + BAND]
    return pl.pallas_call(
        average_kernel,
        grid_spec=pltpu.PrefetchScalarGridSpec(
            num_scalar_prefetch=1,
            grid=(1,),
            in_specs=[
                whole((OWN, SROWS, 128)),
                pl.BlockSpec((1, 128, 128), lambda i, dom: (dom[0], 0, 0)),
            ],
            out_specs=whole((KD * BAND, ROW)),
            scratch_shapes=[pltpu.VMEM((KD * BAND, 128), F32)] * 3,
        ),
        out_shape=jax.ShapeDtypeStruct((KD * BAND, ROW), F32),
        compiler_params=pltpu.CompilerParams(vmem_limit_bytes=VMEM_BYTES),
        cost_estimate=pl.CostEstimate(
            flops=2000000000, bytes_accessed=6000000, transcendentals=0
        ),
        name="averages",
    )(dom, arrived, jnp.asarray(squares))


def on_device(particles, references, class_block, class_local, rotation, shifts, defocus):
    dom = lax.axis_index("dom").astype(jnp.int32).reshape(1)
    core = dom % 2
    full_table, split_table = dft_rows()
    table = jnp.asarray(split_table)
    block = own_harmonics(core, references, table)
    scalars = jnp.stack(
        [shifts[:, 0], shifts[:, 1], defocus, rotation, class_block[:, 0], class_local], axis=0
    )
    rows = particles.reshape(PD * CYC, ROW)

    def spread_of(*blocks):
        *blocks, held = lax.optimization_barrier((*blocks, scalars))
        return *blocks, spread_bands(rows, held, full_table)

    gathered, joined, sums = gather_blocks(block, spread_of)
    late_scalars, _ = lax.optimization_barrier((scalars, joined))
    own, other = weighted_spectra(core, rows, late_scalars, table)
    swap = [(i, i ^ 1) for i in range(DOM)]
    far = lax.ppermute(other, "dom", swap)
    sums = lax.all_to_all(sums, "cls", 0, 0, tiled=True)
    class_average = averages(dom, sums).reshape(KD, BAND, ROW)
    kept, sent, norm = fold(core, gathered, own, far, defocus)
    came = lax.ppermute(sent, "dom", swap)
    best_score = scores(core, kept, came, norm).reshape(PD)
    return (best_score, class_average)


def solution(mesh):
    placed = (
        P(("dom", "cls"), None, None),
        P("cls", None, None),
        P(("dom", "cls"), None),
        P(("dom", "cls")),
        P(("dom", "cls")),
        P(("dom", "cls"), None),
        P(("dom", "cls")),
    )
    return jax.shard_map(
        on_device,
        mesh=mesh,
        in_specs=placed,
        out_specs=(P(("dom", "cls")), P("cls", "dom", None)),
        check_vma=False,
    )
```

profile of v0, /device:TPU:23, one launch (start us, length us, event | category | flops | bytes accessed | tf_op | source)
XLA Modules:
  0.0 111.7 jit_solution(13587210055818749855)
XLA Ops:
  0.6 0.0 copy-start.12
  0.7 0.0 copy-start.13
  0.7 0.0 copy-start.14
  0.7 0.0 copy-start.15
  0.7 0.0 copy-start.16
  0.7 0.0 copy-start.4
  0.7 0.0 copy-start.6
  0.7 0.0 copy-start.7
  0.7 0.0 copy-start.9
  0.7 0.0 copy-start.10
  0.8 4.1 %harmonics.1.refs_0_.refs_17_ = bf16[1920,128]{1,0:T(8,128)(2,1)} custom-call(s32[1]{0:T(128)S(6)} %select_n.7.core, bf16[1600,288]{1,0:T(8,128)(2,1)} %bitcast.24, bf16[2,320,288]{2,1,0:T(8,128)(2,1)} %constant.45.clone.table_any.table, f32[2,128,128]{2,1,0:T(8,128)} %constant.46.clone.squares_any), custom_call_target="tpu_custom_call" | custom-call | flops 4000000000 | bytes 12000000 | tf_op jit(solution)/shard_map/harmonics/pallas_call | solution.py:210
  4.9 1.2 %collective-permute-start.2 = (bf16[1920,128]{1,0:T(8,128)(2,1)}, bf16[1920,128]{1,0:T(8,128)(2,1)S(1)}, u32[]{:S(2)}, u32[]{:S(2)}) collective-permute-start(bf16[1920,128]{1,0:T(8,128)(2,1)} %harmonics.1.refs_0_.refs_17_), channel_id=1, source_target_pairs={{0,8},{1,9},{2,10},{3,11},{4,12},{5,13},{6,14},{7,15},{8,0},{9,1},... | collective-permute-start | bytes 1474568 | tf_op jit(solution)/shard_map/ppermute | solution.py:558
  6.1 3.6 %collective-permute-start.5 = (bf16[1920,128]{1,0:T(8,128)(2,1)}, bf16[1920,128]{1,0:T(8,128)(2,1)}, u32[]{:S(2)}, u32[]{:S(2)}) collective-permute-start(bf16[1920,128]{1,0:T(8,128)(2,1)} %harmonics.1.refs_0_.refs_17_), channel_id=1, source_target_pairs={{0,2},{1,3},{2,0},{3,1},{4,6},{5,7},{6,4},{7,5},{8,10},{9,11},{10,... | collective-permute-start | bytes 1474568 | tf_op jit(solution)/shard_map/ppermute | solution.py:558
  9.7 0.4 collective-permute-start.4
  10.1 1.0 collective-permute-start.3
  11.2 0.0 collective-permute-start.1
  11.2 0.0 copy-done.13
  11.3 7.7 %collective-permute-done.2.two_x.refs_3_.refs_20_ = bf16[1920,128]{1,0:T(8,128)(2,1)S(1)} collective-permute-done((bf16[1920,128]{1,0:T(8,128)(2,1)}, bf16[1920,128]{1,0:T(8,128)(2,1)S(1)}, u32[]{:S(2)}, u32[]{:S(2)}) %collective-permute-start.2) | collective-permute-done | bytes 491552 | tf_op jit(solution)/shard_map/ppermute | solution.py:558
  18.9 0.2 collective-permute-start
  19.1 0.0 copy-start.1
  19.1 1.7 %copy-done.1 = bf16[48,64,288]{2,1,0:T(8,128)(2,1)S(1)} copy-done((bf16[48,64,288]{2,1,0:T(8,128)(2,1)S(1)}, bf16[48,64,288]{2,1,0:T(8,128)(2,1)}, u32[]{:S(2)}) %copy-start.1) | copy-done | bytes 1769496
  20.8 7.9 %spread.1 = bf16[7296,128]{1,0:T(8,128)(2,1)S(1)} custom-call(s32[6,48]{1,0:T(8,128)S(1)} %stack.15.scalars, bf16[3072,288]{1,0:T(8,128)(2,1)S(1)} %bitcast.17, bf16[288,768]{1,0:T(8,128)(2,1)S(1)} %copy-done.6, bf16[288,288]{1,0:T(8,128)(2,1)S(1)} %copy-done.7, f32[4,6,16,288]{3,2,1,0:T(8,128)S(1)} %copy-done.4, f32[36,8,128]{2,1,0:T(8,128)S(1)} %copy-done.9, ...), custom_call_target="tpu_custom_call" | custom-call | flops 8999999488 | bytes 27000000 | tf_op jit(solution)/shard_map/spread/pallas_call | solution.py:321
  28.7 1.3 %copy-done = bf16[7296,128]{1,0:T(8,128)(2,1)} copy-done((bf16[7296,128]{1,0:T(8,128)(2,1)}, bf16[7296,128]{1,0:T(8,128)(2,1)S(1)}, u32[]{:S(2)}) %copy-start) | copy-done | bytes 1867800
  30.0 7.0 %all-to-all-start = ((bf16[8,912,128]{2,1,0:T(8,128)(2,1)}), bf16[8,912,128]{2,1,0:T(8,128)(2,1)S(1)}, u32[]{:S(2)}, u32[]{:S(2)}) async-start(bf16[8,912,128]{2,1,0:T(8,128)(2,1)} %bitcast.16), calls=%async_computation | async-start | bytes 3735552 | tf_op jit(solution)/shard_map/all_to_all | solution.py:646
  37.0 0.0 collective-permute-done.5.two_z.refs_6_.refs_23_
  37.0 0.0 collective-permute-done.4.up.refs_5_.refs_22_
  37.1 0.0 collective-permute-done.3.down.refs_4_.refs_21_
  37.1 0.0 collective-permute-done.1.right.refs_2_.refs_19_
  37.1 0.0 collective-permute-done.left.refs_1_.refs_18_
  37.1 2.4 %join.1 = (bf16[2880,128]{1,0:T(8,128)(2,1)}, bf16[2880,128]{1,0:T(8,128)(2,1)}) custom-call(bf16[1920,128]{1,0:T(8,128)(2,1)} %collective-permute-done.left.refs_1_.refs_18_, bf16[1920,128]{1,0:T(8,128)(2,1)} %collective-permute-done.1.right.refs_2_.refs_19_, bf16[1920,128]{1,0:T(8,128)(2,1)} %copy-done.18, ...), custom_call_target="tpu_custom_call" | custom-call | flops 2000000000 | bytes 6000000 | tf_op jit(solution)/shard_map/join/pallas_call | solution.py:583
  39.5 1.6 %collective-permute-start.9 = (bf16[2880,128]{1,0:T(8,128)(2,1)}, bf16[2880,128]{1,0:T(8,128)(2,1)}, u32[]{:S(2)}, u32[]{:S(2)}) collective-permute-start(bf16[2880,128]{1,0:T(8,128)(2,1)} %get-tuple-element.23), channel_id=1, source_target_pairs={{0,12},{1,13},{2,14},{3,15},{4,0},{5,1},{6,2},{7,3},{8,4},{9,5},{1... | collective-permute-start | bytes 2211848 | tf_op jit(solution)/shard_map/ppermute | solution.py:558
  41.2 1.1 collective-permute-start.8
  42.3 3.8 %collective-permute-start.7 = (bf16[2880,128]{1,0:T(8,128)(2,1)}, bf16[2880,128]{1,0:T(8,128)(2,1)}, u32[]{:S(2)}, u32[]{:S(2)}) collective-permute-start(bf16[2880,128]{1,0:T(8,128)(2,1)} %get-tuple-element.22), channel_id=1, source_target_pairs={{0,3},{1,0},{2,1},{3,2},{4,7},{5,4},{6,5},{7,6},{8,11},{9,8},{10,9... | collective-permute-start | bytes 2211848 | tf_op jit(solution)/shard_map/ppermute | solution.py:558
  46.0 0.0 collective-permute-start.6
  46.0 0.0 copy-start.5
  46.0 1.0 copy-done.5
  47.1 7.3 %weights.1 = (bf16[3456,128]{1,0:T(8,128)(2,1)S(1)}, bf16[3456,128]{1,0:T(8,128)(2,1)S(1)}) custom-call(s32[1]{0:T(128)S(6)} %select_n.7.core, s32[6,48]{1,0:T(8,128)S(1)} %stack.15.scalars, bf16[3072,288]{1,0:T(8,128)(2,1)S(1)} %bitcast.18, bf16[2,320,288]{2,1,0:T(8,128)(2,1)S(1)} %copy-done.5, bf16[288,288]{1,0:T(8,128)(2,1)S(1)} %copy-done.8, ...), custom_call_target="tpu_custom_call" | custom-call | flops 10000000000 | bytes 30000000 | tf_op jit(solution)/shard_map/weights/pallas_call | solution.py:395
  54.4 0.9 copy-done.3
  55.3 1.2 %collective-permute-start.14 = (bf16[3456,128]{1,0:T(8,128)(2,1)S(1)}, bf16[3456,128]{1,0:T(8,128)(2,1)}, u32[]{:S(2)}, u32[]{:S(2)}) collective-permute-start(bf16[3456,128]{1,0:T(8,128)(2,1)S(1)} %get-tuple-element.35), channel_id=1, source_target_pairs={{0,16},{16,0},{32,48},{48,32},{64,80},{80,64},{96,112},{112,96},{1... | collective-permute-start | bytes 2654216 | tf_op jit(solution)/shard_map/ppermute | solution.py:903
  56.5 1.9 %all-to-all-done.arrived = bf16[8,912,128]{2,1,0:T(8,128)(2,1)S(1)} async-done(((bf16[8,912,128]{2,1,0:T(8,128)(2,1)}), bf16[8,912,128]{2,1,0:T(8,128)(2,1)S(1)}, u32[]{:S(2)}, u32[]{:S(2)}) %all-to-all-start) | async-done | bytes 1867808 | tf_op jit(solution)/shard_map/all_to_all | solution.py:646
  58.5 3.0 %class_sums.1 = bf16[16,480,128]{2,1,0:T(8,128)(2,1)} custom-call(bf16[8,912,128]{2,1,0:T(8,128)(2,1)S(1)} %all-to-all-done.arrived), custom_call_target="tpu_custom_call" | custom-call | flops 3000000000 | bytes 9000000 | tf_op jit(solution)/shard_map/class_sums/pallas_call | solution.py:817
  61.5 0.0 collective-permute-done.9.high_after.refs_25_.refs_28_.refs_32_
  61.5 0.0 collective-permute-done.8.high_before.refs_24_.refs_27_.refs_31_
  61.5 0.0 collective-permute-done.7.low_after.refs_8_.refs_11_.refs_15_
  61.5 2.8 %collective-permute-done.6.low_before.refs_7_.refs_10_.refs_14_ = bf16[2880,128]{1,0:T(8,128)(2,1)} collective-permute-done((bf16[2880,128]{1,0:T(8,128)(2,1)}, bf16[2880,128]{1,0:T(8,128)(2,1)}, u32[]{:S(2)}, u32[]{:S(2)}) %collective-permute-start.6) | collective-permute-done | bytes 737312 | tf_op jit(solution)/shard_map/ppermute | solution.py:558
  64.3 2.2 %cut.1 = (bf16[1440,128]{1,0:T(8,128)(2,1)}, bf16[1440,128]{1,0:T(8,128)(2,1)}, bf16[1440,128]{1,0:T(8,128)(2,1)}, bf16[1440,128]{1,0:T(8,128)(2,1)}) custom-call(bf16[2880,128]{1,0:T(8,128)(2,1)} %collective-permute-done.6.low_before.refs_7_.refs_10_.refs_14_, bf16[2880,128]{1,0:T(8,128)(2,1)} %collective-permute-done.7.low_after.refs_8_.refs_11_.refs_15_, ...), custom_call_target="tpu_custom_call" | custom-call | flops 2000000000 | bytes 6000000 | tf_op jit(solution)/shard_map/cut/pallas_call | solution.py:620
  66.5 0.1 collective-permute-start.10
  66.6 2.7 %collective-permute-start.11 = (bf16[1440,128]{1,0:T(8,128)(2,1)}, bf16[1440,128]{1,0:T(8,128)(2,1)S(1)}, u32[]{:S(2)}, u32[]{:S(2)}) collective-permute-start(bf16[1440,128]{1,0:T(8,128)(2,1)} %get-tuple-element.30), channel_id=1, source_target_pairs={{0,3},{1,0},{2,1},{3,2},{4,7},{5,4},{6,5},{7,6},{8,11},{9,8},{10,9... | collective-permute-start | bytes 1105928 | tf_op jit(solution)/shard_map/ppermute | solution.py:558
  69.3 0.3 collective-permute-start.12
  69.6 1.1 %collective-permute-start.13 = (bf16[1440,128]{1,0:T(8,128)(2,1)}, bf16[1440,128]{1,0:T(8,128)(2,1)S(1)}, u32[]{:S(2)}, u32[]{:S(2)}) collective-permute-start(bf16[1440,128]{1,0:T(8,128)(2,1)} %get-tuple-element.32), channel_id=1, source_target_pairs={{0,12},{1,13},{2,14},{3,15},{4,0},{5,1},{6,2},{7,3},{8,4},{9,5},{1... | collective-permute-start | bytes 1105928 | tf_op jit(solution)/shard_map/ppermute | solution.py:558
  70.7 5.8 %all-to-all-start.1 = ((bf16[16,480,128]{2,1,0:T(8,128)(2,1)}), bf16[16,480,128]{2,1,0:T(8,128)(2,1)}, u32[]{:S(2)}, u32[]{:S(2)}) async-start(bf16[16,480,128]{2,1,0:T(8,128)(2,1)} %class_sums.1), calls=%async_computation.1 | async-start | bytes 3932160 | tf_op jit(solution)/shard_map/all_to_all | solution.py:904
  76.5 0.0 collective-permute-done.14
  76.5 0.0 collective-permute-done.10.refs_9_.refs_12_
  76.5 0.0 collective-permute-done.11.refs_13_.refs_16_
  76.6 0.3 collective-permute-done.12.refs_26_.refs_29_
  76.9 1.3 %collective-permute-done.13.refs_30_.refs_33_ = bf16[1440,128]{1,0:T(8,128)(2,1)S(1)} collective-permute-done((bf16[1440,128]{1,0:T(8,128)(2,1)}, bf16[1440,128]{1,0:T(8,128)(2,1)S(1)}, u32[]{:S(2)}, u32[]{:S(2)}) %collective-permute-start.13) | collective-permute-done | bytes 368672 | tf_op jit(solution)/shard_map/ppermute | solution.py:558
  78.1 0.7 copy-done.22
  78.9 9.5 %fold.1 = (bf16[18,48,512]{2,1,0:T(8,128)(2,1)}, bf16[18,48,512]{2,1,0:T(8,128)(2,1)}, f32[48,512]{1,0:T(8,128)}) custom-call(s32[1]{0:T(128)S(6)} %select_n.7.core, bf16[1920,128]{1,0:T(8,128)(2,1)} %harmonics.1.refs_0_.refs_17_, bf16[1920,128]{1,0:T(8,128)(2,1)} %collective-permute-done.left.refs_1_.refs_18_, ...), custom_call_target="tpu_custom_call" | custom-call | flops 8999999488 | bytes 27000000 | tf_op jit(solution)/shard_map/fold/pallas_call | solution.py:521
  88.4 13.4 %collective-permute-start.15 = (bf16[18,48,512]{2,1,0:T(8,128)(2,1)}, bf16[18,48,512]{2,1,0:T(8,128)(2,1)S(1)}, u32[]{:S(2)}, u32[]{:S(2)}) collective-permute-start(bf16[18,48,512]{2,1,0:T(8,128)(2,1)} %get-tuple-element.37), channel_id=1, source_target_pairs={{0,16},{16,0},{32,48},{48,32},{64,80},{80,64},{96,112},{112,96},{1... | collective-permute-start | bytes 2654216 | tf_op jit(solution)/shard_map/ppermute | solution.py:907
  101.8 2.3 %collective-permute-done.15.came = bf16[18,48,512]{2,1,0:T(8,128)(2,1)S(1)} collective-permute-done((bf16[18,48,512]{2,1,0:T(8,128)(2,1)}, bf16[18,48,512]{2,1,0:T(8,128)(2,1)S(1)}, u32[]{:S(2)}, u32[]{:S(2)}) %collective-permute-start.15) | collective-permute-done | bytes 884768 | tf_op jit(solution)/shard_map/ppermute | solution.py:907
  104.0 0.9 copy-done.17
  105.0 3.9 %scores.1 = f32[1,48]{1,0:T(1,128)} custom-call(s32[1]{0:T(128)S(6)} %select_n.7.core, bf16[18,48,512]{2,1,0:T(8,128)(2,1)} %get-tuple-element.36.kept, bf16[18,48,512]{2,1,0:T(8,128)(2,1)} %copy-done.17, f32[48,512]{1,0:T(8,128)} %get-tuple-element.38.norm), custom_call_target="tpu_custom_call" | custom-call | flops 3000000000 | bytes 9000000 | tf_op jit(solution)/shard_map/scores/pallas_call | solution.py:766
  108.9 0.0 all-to-all-done.1.arrived
  108.9 2.8 %averages.1 = f32[200,288]{1,0:T(8,128)} custom-call(s32[1]{0:T(128)} %bitcast.dom, bf16[16,480,128]{2,1,0:T(8,128)(2,1)} %all-to-all-done.1.arrived, f32[8,128,128]{2,1,0:T(8,128)} %constant.53.clone.squares), custom_call_target="tpu_custom_call" | custom-call | flops 2000000000 | bytes 6000000 | tf_op jit(solution)/shard_map/averages/pallas_call | solution.py:863
  (29 shorter events, 0.1 us)
Async XLA Ops:
  0.6 10.5 %copy-start.12 = (s32[48,2]{0,1:T(2,128)S(1)}, s32[48,2]{0,1:T(2,128)}, u32[]{:S(2)}) copy-start(s32[48,2]{0,1:T(2,128)} %param.24) | copy-start | bytes 1156
  0.7 10.5 %copy-start.13 = (s32[48]{0:T(128)S(1)}, s32[48]{0:T(128)}, u32[]{:S(2)}) copy-start(s32[48]{0:T(128)} %param.23) | copy-start | bytes 580
  0.7 10.5 %copy-start.14 = (s32[48,1]{0,1:T(1,128)S(1)}, s32[48,1]{0,1:T(1,128)}, u32[]{:S(2)}) copy-start(s32[48,1]{0,1:T(1,128)} %param.21) | copy-start | bytes 580
  0.7 10.5 %copy-start.15 = (s32[48]{0:T(128)S(1)}, s32[48]{0:T(128)}, u32[]{:S(2)}) copy-start(s32[48]{0:T(128)} %param.22) | copy-start | bytes 580
  0.7 10.5 %copy-start.16 = (s32[48]{0:T(128)S(1)}, s32[48]{0:T(128)}, u32[]{:S(2)}) copy-start(s32[48]{0:T(128)} %refs_37_.1) | copy-start | bytes 580
  0.7 18.4 %copy-start.4 = (f32[4,6,16,288]{3,2,1,0:T(8,128)S(1)}, f32[4,6,16,288]{3,2,1,0:T(8,128)}, u32[]{:S(2)}) copy-start(f32[4,6,16,288]{3,2,1,0:T(8,128)} %constant.49.clone.phases) | copy-start | bytes 1327108
  0.7 18.4 %copy-start.6 = (bf16[288,768]{1,0:T(8,128)(2,1)S(1)}, bf16[288,768]{1,0:T(8,128)(2,1)}, u32[]{:S(2)}) copy-start(bf16[288,768]{1,0:T(8,128)(2,1)} %constant.47.clone.wide) | copy-start | bytes 1327108
  0.7 18.4 %copy-start.7 = (bf16[288,288]{1,0:T(8,128)(2,1)S(1)}, bf16[288,288]{1,0:T(8,128)(2,1)}, u32[]{:S(2)}) copy-start(bf16[288,288]{1,0:T(8,128)(2,1)} %constant.48.clone.swap) | copy-start | bytes 497668
  0.7 18.4 %copy-start.9 = (f32[36,8,128]{2,1,0:T(8,128)S(1)}, f32[36,8,128]{2,1,0:T(8,128)}, u32[]{:S(2)}) copy-start(f32[36,8,128]{2,1,0:T(8,128)} %constant.50.clone.turn) | copy-start | bytes 442372
  0.7 18.4 %copy-start.10 = (f32[64,128]{1,0:T(8,128)S(1)}, f32[64,128]{1,0:T(8,128)}, u32[]{:S(2)}) copy-start(f32[64,128]{1,0:T(8,128)} %constant.51.clone.ctf_columns) | copy-start | bytes 98308
  4.9 14.0 %collective-permute-start.2 = (bf16[1920,128]{1,0:T(8,128)(2,1)}, bf16[1920,128]{1,0:T(8,128)(2,1)S(1)}, u32[]{:S(2)}, u32[]{:S(2)}) collective-permute-start(bf16[1920,128]{1,0:T(8,128)(2,1)} %harmonics.1.refs_0_.refs_17_), channel_id=1, source_target_pairs={{0,8},{1,9},{2,10},{3,11},{4,12},{5,13},{6,14},{7,15},{8,0},{9,1},... | collective-permute-start | bytes 1474568 | tf_op jit(solution)/shard_map/ppermute | solution.py:558
  6.1 30.9 %collective-permute-start.5 = (bf16[1920,128]{1,0:T(8,128)(2,1)}, bf16[1920,128]{1,0:T(8,128)(2,1)}, u32[]{:S(2)}, u32[]{:S(2)}) collective-permute-start(bf16[1920,128]{1,0:T(8,128)(2,1)} %harmonics.1.refs_0_.refs_17_), channel_id=1, source_target_pairs={{0,2},{1,3},{2,0},{3,1},{4,6},{5,7},{6,4},{7,5},{8,10},{9,11},{10,... | collective-permute-start | bytes 1474568 | tf_op jit(solution)/shard_map/ppermute | solution.py:558
  9.7 27.3 %collective-permute-start.4 = (bf16[1920,128]{1,0:T(8,128)(2,1)}, bf16[1920,128]{1,0:T(8,128)(2,1)}, u32[]{:S(2)}, u32[]{:S(2)}) collective-permute-start(bf16[1920,128]{1,0:T(8,128)(2,1)} %harmonics.1.refs_0_.refs_17_), channel_id=1, source_target_pairs={{0,3},{1,0},{2,1},{3,2},{4,7},{5,4},{6,5},{7,6},{8,11},{9,8},{10,9... | collective-permute-start | bytes 1474568 | tf_op jit(solution)/shard_map/ppermute | solution.py:558
  10.1 26.9 %collective-permute-start.3 = (bf16[1920,128]{1,0:T(8,128)(2,1)}, bf16[1920,128]{1,0:T(8,128)(2,1)}, u32[]{:S(2)}, u32[]{:S(2)}) collective-permute-start(bf16[1920,128]{1,0:T(8,128)(2,1)} %harmonics.1.refs_0_.refs_17_), channel_id=1, source_target_pairs={{0,1},{1,2},{2,3},{3,0},{4,5},{5,6},{6,7},{7,4},{8,9},{9,10},{10,1... | collective-permute-start | bytes 1474568 | tf_op jit(solution)/shard_map/ppermute | solution.py:558
  11.2 25.9 %collective-permute-start.1 = (bf16[1920,128]{1,0:T(8,128)(2,1)}, bf16[1920,128]{1,0:T(8,128)(2,1)}, u32[]{:S(2)}, u32[]{:S(2)}) collective-permute-start(bf16[1920,128]{1,0:T(8,128)(2,1)} %harmonics.1.refs_0_.refs_17_), channel_id=1, source_target_pairs={{0,12},{1,13},{2,14},{3,15},{4,0},{5,1},{6,2},{7,3},{8,4},{9,5},{1... | collective-permute-start | bytes 1474568 | tf_op jit(solution)/shard_map/ppermute | solution.py:558
  18.9 9.8 %copy-start.18 = (bf16[1920,128]{1,0:T(8,128)(2,1)}, bf16[1920,128]{1,0:T(8,128)(2,1)S(1)}, u32[]{:S(2)}) copy-start(bf16[1920,128]{1,0:T(8,128)(2,1)S(1)} %collective-permute-done.2.two_x.refs_3_.refs_20_) | copy-start | bytes 1474564
  18.9 18.1 %collective-permute-start = (bf16[1920,128]{1,0:T(8,128)(2,1)}, bf16[1920,128]{1,0:T(8,128)(2,1)}, u32[]{:S(2)}, u32[]{:S(2)}) collective-permute-start(bf16[1920,128]{1,0:T(8,128)(2,1)} %harmonics.1.refs_0_.refs_17_), channel_id=1, source_target_pairs={{0,4},{1,5},{2,6},{3,7},{4,8},{5,9},{6,10},{7,11},{8,12},{9,13},{1... | collective-permute-start | bytes 1474568 | tf_op jit(solution)/shard_map/ppermute | solution.py:558
  19.1 1.7 %copy-start.1 = (bf16[48,64,288]{2,1,0:T(8,128)(2,1)S(1)}, bf16[48,64,288]{2,1,0:T(8,128)(2,1)}, u32[]{:S(2)}) copy-start(bf16[48,64,288]{2,1,0:T(8,128)(2,1)} %param.19) | copy-start | bytes 5308420
  28.7 1.3 %copy-start = (bf16[7296,128]{1,0:T(8,128)(2,1)}, bf16[7296,128]{1,0:T(8,128)(2,1)S(1)}, u32[]{:S(2)}) copy-start(bf16[7296,128]{1,0:T(8,128)(2,1)S(1)} %spread.1) | copy-start | bytes 5603332
  30.0 28.5 %all-to-all-start = ((bf16[8,912,128]{2,1,0:T(8,128)(2,1)}), bf16[8,912,128]{2,1,0:T(8,128)(2,1)S(1)}, u32[]{:S(2)}, u32[]{:S(2)}) async-start(bf16[8,912,128]{2,1,0:T(8,128)(2,1)} %bitcast.16), calls=%async_computation | async-start | bytes 3735552 | tf_op jit(solution)/shard_map/all_to_all | solution.py:646
  37.0 9.0 %copy-start.2 = (bf16[48,64,288]{2,1,0:T(8,128)(2,1)S(1)}, bf16[48,64,288]{2,1,0:T(8,128)(2,1)}, u32[]{:S(2)}) copy-start(bf16[48,64,288]{2,1,0:T(8,128)(2,1)} %param.19) | copy-start | bytes 5308420
  37.0 9.0 %copy-start.8 = (bf16[288,288]{1,0:T(8,128)(2,1)S(1)}, bf16[288,288]{1,0:T(8,128)(2,1)}, u32[]{:S(2)}) copy-start(bf16[288,288]{1,0:T(8,128)(2,1)} %constant.48.clone.swap) | copy-start | bytes 497668
  37.0 9.0 %copy-start.11 = (f32[16,128]{1,0:T(8,128)S(1)}, f32[16,128]{1,0:T(8,128)}, u32[]{:S(2)}) copy-start(f32[16,128]{1,0:T(8,128)} %constant.52.clone.ctf_rows) | copy-start | bytes 24580
  39.5 22.0 %collective-permute-start.9 = (bf16[2880,128]{1,0:T(8,128)(2,1)}, bf16[2880,128]{1,0:T(8,128)(2,1)}, u32[]{:S(2)}, u32[]{:S(2)}) collective-permute-start(bf16[2880,128]{1,0:T(8,128)(2,1)} %get-tuple-element.23), channel_id=1, source_target_pairs={{0,12},{1,13},{2,14},{3,15},{4,0},{5,1},{6,2},{7,3},{8,4},{9,5},{1... | collective-permute-start | bytes 2211848 | tf_op jit(solution)/shard_map/ppermute | solution.py:558
  41.2 20.3 %collective-permute-start.8 = (bf16[2880,128]{1,0:T(8,128)(2,1)}, bf16[2880,128]{1,0:T(8,128)(2,1)}, u32[]{:S(2)}, u32[]{:S(2)}) collective-permute-start(bf16[2880,128]{1,0:T(8,128)(2,1)} %get-tuple-element.23), channel_id=1, source_target_pairs={{0,4},{1,5},{2,6},{3,7},{4,8},{5,9},{6,10},{7,11},{8,12},{9,13},{1... | collective-permute-start | bytes 2211848 | tf_op jit(solution)/shard_map/ppermute | solution.py:558
  42.3 19.2 %collective-permute-start.7 = (bf16[2880,128]{1,0:T(8,128)(2,1)}, bf16[2880,128]{1,0:T(8,128)(2,1)}, u32[]{:S(2)}, u32[]{:S(2)}) collective-permute-start(bf16[2880,128]{1,0:T(8,128)(2,1)} %get-tuple-element.22), channel_id=1, source_target_pairs={{0,3},{1,0},{2,1},{3,2},{4,7},{5,4},{6,5},{7,6},{8,11},{9,8},{10,9... | collective-permute-start | bytes 2211848 | tf_op jit(solution)/shard_map/ppermute | solution.py:558
  46.0 18.3 %collective-permute-start.6 = (bf16[2880,128]{1,0:T(8,128)(2,1)}, bf16[2880,128]{1,0:T(8,128)(2,1)}, u32[]{:S(2)}, u32[]{:S(2)}) collective-permute-start(bf16[2880,128]{1,0:T(8,128)(2,1)} %get-tuple-element.22), channel_id=1, source_target_pairs={{0,1},{1,2},{2,3},{3,0},{4,5},{5,6},{6,7},{7,4},{8,9},{9,10},{10,1... | collective-permute-start | bytes 2211848 | tf_op jit(solution)/shard_map/ppermute | solution.py:558
  46.0 1.0 copy-start.5
  54.4 0.9 copy-start.3
  55.3 21.2 %collective-permute-start.14 = (bf16[3456,128]{1,0:T(8,128)(2,1)S(1)}, bf16[3456,128]{1,0:T(8,128)(2,1)}, u32[]{:S(2)}, u32[]{:S(2)}) collective-permute-start(bf16[3456,128]{1,0:T(8,128)(2,1)S(1)} %get-tuple-element.35), channel_id=1, source_target_pairs={{0,16},{16,0},{32,48},{48,32},{64,80},{80,64},{96,112},{112,96},{1... | collective-permute-start | bytes 2654216 | tf_op jit(solution)/shard_map/ppermute | solution.py:903
  66.5 10.0 %collective-permute-start.10 = (bf16[1440,128]{1,0:T(8,128)(2,1)}, bf16[1440,128]{1,0:T(8,128)(2,1)S(1)}, u32[]{:S(2)}, u32[]{:S(2)}) collective-permute-start(bf16[1440,128]{1,0:T(8,128)(2,1)} %get-tuple-element.29), channel_id=1, source_target_pairs={{0,1},{1,2},{2,3},{3,0},{4,5},{5,6},{6,7},{7,4},{8,9},{9,10},{10,1... | collective-permute-start | bytes 1105928 | tf_op jit(solution)/shard_map/ppermute | solution.py:558
  66.6 9.9 %collective-permute-start.11 = (bf16[1440,128]{1,0:T(8,128)(2,1)}, bf16[1440,128]{1,0:T(8,128)(2,1)S(1)}, u32[]{:S(2)}, u32[]{:S(2)}) collective-permute-start(bf16[1440,128]{1,0:T(8,128)(2,1)} %get-tuple-element.30), channel_id=1, source_target_pairs={{0,3},{1,0},{2,1},{3,2},{4,7},{5,4},{6,5},{7,6},{8,11},{9,8},{10,9... | collective-permute-start | bytes 1105928 | tf_op jit(solution)/shard_map/ppermute | solution.py:558
  69.3 7.6 %collective-permute-start.12 = (bf16[1440,128]{1,0:T(8,128)(2,1)}, bf16[1440,128]{1,0:T(8,128)(2,1)S(1)}, u32[]{:S(2)}, u32[]{:S(2)}) collective-permute-start(bf16[1440,128]{1,0:T(8,128)(2,1)} %get-tuple-element.31), channel_id=1, source_target_pairs={{0,4},{1,5},{2,6},{3,7},{4,8},{5,9},{6,10},{7,11},{8,12},{9,13},{1... | collective-permute-start | bytes 1105928 | tf_op jit(solution)/shard_map/ppermute | solution.py:558
  69.6 8.5 %collective-permute-start.13 = (bf16[1440,128]{1,0:T(8,128)(2,1)}, bf16[1440,128]{1,0:T(8,128)(2,1)S(1)}, u32[]{:S(2)}, u32[]{:S(2)}) collective-permute-start(bf16[1440,128]{1,0:T(8,128)(2,1)} %get-tuple-element.32), channel_id=1, source_target_pairs={{0,12},{1,13},{2,14},{3,15},{4,0},{5,1},{6,2},{7,3},{8,4},{9,5},{1... | collective-permute-start | bytes 1105928 | tf_op jit(solution)/shard_map/ppermute | solution.py:558
  70.7 38.2 %all-to-all-start.1 = ((bf16[16,480,128]{2,1,0:T(8,128)(2,1)}), bf16[16,480,128]{2,1,0:T(8,128)(2,1)}, u32[]{:S(2)}, u32[]{:S(2)}) async-start(bf16[16,480,128]{2,1,0:T(8,128)(2,1)} %class_sums.1), calls=%async_computation.1 | async-start | bytes 3932160 | tf_op jit(solution)/shard_map/all_to_all | solution.py:904
  76.5 1.6 %copy-start.19 = (bf16[1440,128]{1,0:T(8,128)(2,1)}, bf16[1440,128]{1,0:T(8,128)(2,1)S(1)}, u32[]{:S(2)}) copy-start(bf16[1440,128]{1,0:T(8,128)(2,1)S(1)} %collective-permute-done.10.refs_9_.refs_12_) | copy-start | bytes 1105924
  76.5 1.6 %copy-start.20 = (bf16[1440,128]{1,0:T(8,128)(2,1)}, bf16[1440,128]{1,0:T(8,128)(2,1)S(1)}, u32[]{:S(2)}) copy-start(bf16[1440,128]{1,0:T(8,128)(2,1)S(1)} %collective-permute-done.11.refs_13_.refs_16_) | copy-start | bytes 1105924
  76.9 1.3 %copy-start.21 = (bf16[1440,128]{1,0:T(8,128)(2,1)}, bf16[1440,128]{1,0:T(8,128)(2,1)S(1)}, u32[]{:S(2)}) copy-start(bf16[1440,128]{1,0:T(8,128)(2,1)S(1)} %collective-permute-done.12.refs_26_.refs_29_) | copy-start | bytes 1105924
  78.1 0.7 copy-start.22
  88.4 15.6 %collective-permute-start.15 = (bf16[18,48,512]{2,1,0:T(8,128)(2,1)}, bf16[18,48,512]{2,1,0:T(8,128)(2,1)S(1)}, u32[]{:S(2)}, u32[]{:S(2)}) collective-permute-start(bf16[18,48,512]{2,1,0:T(8,128)(2,1)} %get-tuple-element.37), channel_id=1, source_target_pairs={{0,16},{16,0},{32,48},{48,32},{64,80},{80,64},{96,112},{112,96},{1... | collective-permute-start | bytes 2654216 | tf_op jit(solution)/shard_map/ppermute | solution.py:907
  104.0 0.9 copy-start.17
where the time goes:
time: 112 us
  starting transfers between devices  44.5 us (40%)
  Pallas kernels  43.2 us (39%)
  waiting for transfers between devices  16.3 us (15%)
  local copies, waits for them, and re-layouts  6.66 us (6%)
    ppermute x14, starting transfers between devices, moved_by(): return lax.ppermute(value, 'cls', moves)  17.2 us
    ppermute x1, starting transfers between devices, on_device(): came = lax.ppermute(sent, 'dom', swap)  13.4 us
    ppermute x14, waiting for transfers between devices, moved_by(): return lax.ppermute(value, 'cls', moves)  12.1 us
    pallas_call x1, Pallas kernels, fold(): pl.pallas_call(functools.partial(fold_kernel, layout, count), in_specs=[p...  9.54 us
    pallas_call x1, Pallas kernels, spread_bands(): pl.pallas_call(spread_kernel, grid_spec=pltpu.PrefetchScalarGridSpec(num_...  7.89 us
    pallas_call x1, Pallas kernels, weighted_spectra(): pl.pallas_call(weight_kernel, grid_spec=pltpu.PrefetchScalarGridSpec(num_...  7.34 us
    all_to_all x1, starting transfers between devices, gather_blocks(): lax.all_to_all(spread.reshape(DOM, UROWS, 128), 'dom', 0, 0, tiled=True)  7.02 us
    unnamed x46, local copies, waits for them, and re-layouts  6.63 us
  transfers between devices with their start and end apart: 18, of which 6 were waited for; matrix products, arithmetic and copies ran while one was open for 0% of the time, Pallas kernels for 32%

commit v1 on v0

--- a/solution.py
+++ b/solution.py
@@ -777,7 +777,7 @@
             scratch_shapes=[pltpu.VMEM((PD, 128), F32)],
         ),
         out_shape=jax.ShapeDtypeStruct((1, PD), F32),
-        compiler_params=pltpu.CompilerParams(vmem_limit_bytes=VMEM_BYTES),
+        compiler_params=pltpu.CompilerParams(vmem_limit_bytes=VMEM_BYTES // 2),
         cost_estimate=pl.CostEstimate(
             flops=3000000000, bytes_accessed=9000000, transcendentals=0
         ),
@@ -873,7 +873,7 @@
             scratch_shapes=[pltpu.VMEM((KD * BAND, 128), F32)] * 3,
         ),
         out_shape=jax.ShapeDtypeStruct((KD * BAND, ROW), F32),
-        compiler_params=pltpu.CompilerParams(vmem_limit_bytes=VMEM_BYTES),
+        compiler_params=pltpu.CompilerParams(vmem_limit_bytes=VMEM_BYTES // 2),
         cost_estimate=pl.CostEstimate(
             flops=2000000000, bytes_accessed=6000000, transcendentals=0
         ),

time: 112 us -> 111 us (level)
  Pallas kernels: 43.2 us -> 40.4 us
    pallas_call x1, Pallas kernels: 2.78 us -> 1.22 us  [averages(): pl.pallas_call(average_kernel, grid_spec=pltpu.PrefetchScalarGridSpec(num...]
    pallas_call x1, Pallas kernels: 3.93 us -> 2.6 us  [scores(): pl.pallas_call(score_kernel, grid_spec=pltpu.PrefetchScalarGridSpec(num_s...]
    unnamed x46 -> x44, local copies, waits for them, and re-layouts: 6.63 us -> 7.03 us
  transfers between devices with their start and end apart: 18 -> 18, of which waited for: 6 -> 7; matrix products, arithmetic and copies ran while one was open for 0% -> 0% of each run, Pallas kernels for 32% -> 32%
where the time goes in v1:
time: 111 us; the launch traced here: 110 us
  starting transfers between devices  44.5 us (40%)
  Pallas kernels  40.4 us (36%)
  waiting for transfers between devices  17.1 us (15%)
  local copies, waits for them, and re-layouts  7.06 us (6%)
    ppermute x14, starting transfers between devices, moved_by(): return lax.ppermute(value, 'cls', moves)  17.2 us
    ppermute x1, starting transfers between devices, on_device(): came = lax.ppermute(sent, 'dom', swap)  14.1 us
    ppermute x14, waiting for transfers between devices, moved_by(): return lax.ppermute(value, 'cls', moves)  13 us
    pallas_call x1, Pallas kernels, fold(): pl.pallas_call(functools.partial(fold_kernel, layout, count), in_specs=[p...  9.55 us
    pallas_call x1, Pallas kernels, spread_bands(): pl.pallas_call(spread_kernel, grid_spec=pltpu.PrefetchScalarGridSpec(num_...  7.9 us
    pallas_call x1, Pallas kernels, weighted_spectra(): pl.pallas_call(weight_kernel, grid_spec=pltpu.PrefetchScalarGridSpec(num_...  7.33 us
    unnamed x44, local copies, waits for them, and re-layouts  7.03 us
    all_to_all x1, starting transfers between devices, gather_blocks(): lax.all_to_all(spread.reshape(DOM, UROWS, 128), 'dom', 0, 0, tiled=True)  7.01 us
  transfers between devices with their start and end apart: 18, of which 7 were waited for; matrix products, arithmetic and copies ran while one was open for 0% of the time, Pallas kernels for 32%

profile of v1, /device:TPU:23, one launch (start us, length us, event | category | flops | bytes accessed | tf_op | source)
XLA Modules:
  0.0 110.1 jit_solution(14615882960437231784)
XLA Ops:
  0.7 0.0 copy-start.19
  0.7 0.0 copy-start.4
  0.7 0.0 copy-start.7
  0.7 0.0 copy-start.8
  0.7 0.0 copy-start.10
  0.7 0.0 copy-start.11
  0.8 4.2 %harmonics.1.refs_0_.refs_17_ = bf16[1920,128]{1,0:T(8,128)(2,1)} custom-call(s32[1]{0:T(128)S(6)} %select_n.7.core, bf16[1600,288]{1,0:T(8,128)(2,1)} %bitcast.24, bf16[2,320,288]{2,1,0:T(8,128)(2,1)} %constant.45.clone.table_any.table, f32[2,128,128]{2,1,0:T(8,128)} %constant.46.clone.squares_any), custom_call_target="tpu_custom_call" | custom-call | flops 4000000000 | bytes 12000000 | tf_op jit(solution)/shard_map/harmonics/pallas_call | solution.py:210
  4.9 1.2 %collective-permute-start.2 = (bf16[1920,128]{1,0:T(8,128)(2,1)}, bf16[1920,128]{1,0:T(8,128)(2,1)S(1)}, u32[]{:S(2)}, u32[]{:S(2)}) collective-permute-start(bf16[1920,128]{1,0:T(8,128)(2,1)} %harmonics.1.refs_0_.refs_17_), channel_id=1, source_target_pairs={{0,8},{1,9},{2,10},{3,11},{4,12},{5,13},{6,14},{7,15},{8,0},{9,1},... | collective-permute-start | bytes 1474568 | tf_op jit(solution)/shard_map/ppermute | solution.py:558
  6.1 3.6 %collective-permute-start.5 = (bf16[1920,128]{1,0:T(8,128)(2,1)}, bf16[1920,128]{1,0:T(8,128)(2,1)}, u32[]{:S(2)}, u32[]{:S(2)}) collective-permute-start(bf16[1920,128]{1,0:T(8,128)(2,1)} %harmonics.1.refs_0_.refs_17_), channel_id=1, source_target_pairs={{0,2},{1,3},{2,0},{3,1},{4,6},{5,7},{6,4},{7,5},{8,10},{9,11},{10,... | collective-permute-start | bytes 1474568 | tf_op jit(solution)/shard_map/ppermute | solution.py:558
  9.8 0.4 collective-permute-start.4
  10.2 1.0 collective-permute-start.3
  11.2 0.0 collective-permute-start.1
  11.2 0.0 copy-done.16
  11.2 0.0 copy-done.17
  11.3 0.0 copy-done.18
  11.3 0.0 copy-done.19
  11.3 7.7 %collective-permute-done.2.two_x.refs_3_.refs_20_ = bf16[1920,128]{1,0:T(8,128)(2,1)S(1)} collective-permute-done((bf16[1920,128]{1,0:T(8,128)(2,1)}, bf16[1920,128]{1,0:T(8,128)(2,1)S(1)}, u32[]{:S(2)}, u32[]{:S(2)}) %collective-permute-start.2) | collective-permute-done | bytes 491552 | tf_op jit(solution)/shard_map/ppermute | solution.py:558
  19.0 0.2 collective-permute-start
  19.1 0.0 copy-done.7
  19.2 0.0 copy-start.1
  19.2 1.7 %copy-done.1 = bf16[48,64,288]{2,1,0:T(8,128)(2,1)S(1)} copy-done((bf16[48,64,288]{2,1,0:T(8,128)(2,1)S(1)}, bf16[48,64,288]{2,1,0:T(8,128)(2,1)}, u32[]{:S(2)}) %copy-start.1) | copy-done | bytes 1769496
  20.8 7.9 %spread.1 = bf16[7296,128]{1,0:T(8,128)(2,1)S(1)} custom-call(s32[6,48]{1,0:T(8,128)S(1)} %stack.15.scalars, bf16[3072,288]{1,0:T(8,128)(2,1)S(1)} %bitcast.17, bf16[288,768]{1,0:T(8,128)(2,1)S(1)} %copy-done.7, bf16[288,288]{1,0:T(8,128)(2,1)S(1)} %copy-done.8, f32[4,6,16,288]{3,2,1,0:T(8,128)S(1)} %copy-done.4, f32[36,8,128]{2,1,0:T(8,128)S(1)} %copy-done.10, ...), custom_call_target="tpu_custom_call" | custom-call | flops 8999999488 | bytes 27000000 | tf_op jit(solution)/shard_map/spread/pallas_call | solution.py:321
  28.8 1.3 %copy-done = bf16[7296,128]{1,0:T(8,128)(2,1)} copy-done((bf16[7296,128]{1,0:T(8,128)(2,1)}, bf16[7296,128]{1,0:T(8,128)(2,1)S(1)}, u32[]{:S(2)}) %copy-start) | copy-done | bytes 1867800
  30.0 7.0 %all-to-all-start = ((bf16[8,912,128]{2,1,0:T(8,128)(2,1)}), bf16[8,912,128]{2,1,0:T(8,128)(2,1)S(1)}, u32[]{:S(2)}, u32[]{:S(2)}) async-start(bf16[8,912,128]{2,1,0:T(8,128)(2,1)} %bitcast.16), calls=%async_computation | async-start | bytes 3735552 | tf_op jit(solution)/shard_map/all_to_all | solution.py:646
  37.1 0.0 collective-permute-done.5.two_z.refs_6_.refs_23_
  37.1 0.0 collective-permute-done.4.up.refs_5_.refs_22_
  37.1 0.0 collective-permute-done.3.down.refs_4_.refs_21_
  37.1 0.0 collective-permute-done.1.right.refs_2_.refs_19_
  37.1 0.0 collective-permute-done.left.refs_1_.refs_18_
  37.1 2.5 %join.1 = (bf16[2880,128]{1,0:T(8,128)(2,1)}, bf16[2880,128]{1,0:T(8,128)(2,1)}) custom-call(bf16[1920,128]{1,0:T(8,128)(2,1)} %collective-permute-done.left.refs_1_.refs_18_, bf16[1920,128]{1,0:T(8,128)(2,1)} %collective-permute-done.1.right.refs_2_.refs_19_, bf16[1920,128]{1,0:T(8,128)(2,1)} %copy-done.20, ...), custom_call_target="tpu_custom_call" | custom-call | flops 2000000000 | bytes 6000000 | tf_op jit(solution)/shard_map/join/pallas_call | solution.py:583
  39.6 1.7 %collective-permute-start.9 = (bf16[2880,128]{1,0:T(8,128)(2,1)}, bf16[2880,128]{1,0:T(8,128)(2,1)}, u32[]{:S(2)}, u32[]{:S(2)}) collective-permute-start(bf16[2880,128]{1,0:T(8,128)(2,1)} %get-tuple-element.23), channel_id=1, source_target_pairs={{0,12},{1,13},{2,14},{3,15},{4,0},{5,1},{6,2},{7,3},{8,4},{9,5},{1... | collective-permute-start | bytes 2211848 | tf_op jit(solution)/shard_map/ppermute | solution.py:558
  41.3 1.1 collective-permute-start.8
  42.3 3.8 %collective-permute-start.7 = (bf16[2880,128]{1,0:T(8,128)(2,1)}, bf16[2880,128]{1,0:T(8,128)(2,1)}, u32[]{:S(2)}, u32[]{:S(2)}) collective-permute-start(bf16[2880,128]{1,0:T(8,128)(2,1)} %get-tuple-element.22), channel_id=1, source_target_pairs={{0,3},{1,0},{2,1},{3,2},{4,7},{5,4},{6,5},{7,6},{8,11},{9,8},{10,9... | collective-permute-start | bytes 2211848 | tf_op jit(solution)/shard_map/ppermute | solution.py:558
  46.1 0.0 collective-permute-start.6
  46.1 0.0 copy-start.6
  46.1 1.0 copy-done.6
  47.2 7.3 %weights.1 = (bf16[3456,128]{1,0:T(8,128)(2,1)S(1)}, bf16[3456,128]{1,0:T(8,128)(2,1)S(1)}) custom-call(s32[1]{0:T(128)S(6)} %select_n.7.core, s32[6,48]{1,0:T(8,128)S(1)} %stack.15.scalars, bf16[3072,288]{1,0:T(8,128)(2,1)S(1)} %bitcast.18, bf16[2,320,288]{2,1,0:T(8,128)(2,1)S(1)} %copy-done.6, bf16[288,288]{1,0:T(8,128)(2,1)S(1)} %copy-done.9, ...), custom_call_target="tpu_custom_call" | custom-call | flops 10000000000 | bytes 30000000 | tf_op jit(solution)/shard_map/weights/pallas_call | solution.py:395
  54.5 0.9 copy-done.3
  55.4 1.2 %collective-permute-start.14 = (bf16[3456,128]{1,0:T(8,128)(2,1)S(1)}, bf16[3456,128]{1,0:T(8,128)(2,1)}, u32[]{:S(2)}, u32[]{:S(2)}) collective-permute-start(bf16[3456,128]{1,0:T(8,128)(2,1)S(1)} %get-tuple-element.35), channel_id=1, source_target_pairs={{0,16},{16,0},{32,48},{48,32},{64,80},{80,64},{96,112},{112,96},{1... | collective-permute-start | bytes 2654216 | tf_op jit(solution)/shard_map/ppermute | solution.py:903
  56.6 1.9 %all-to-all-done.arrived = bf16[8,912,128]{2,1,0:T(8,128)(2,1)S(1)} async-done(((bf16[8,912,128]{2,1,0:T(8,128)(2,1)}), bf16[8,912,128]{2,1,0:T(8,128)(2,1)S(1)}, u32[]{:S(2)}, u32[]{:S(2)}) %all-to-all-start) | async-done | bytes 1867808 | tf_op jit(solution)/shard_map/all_to_all | solution.py:646
  58.5 3.0 %class_sums.1 = bf16[16,480,128]{2,1,0:T(8,128)(2,1)} custom-call(bf16[8,912,128]{2,1,0:T(8,128)(2,1)S(1)} %all-to-all-done.arrived), custom_call_target="tpu_custom_call" | custom-call | flops 3000000000 | bytes 9000000 | tf_op jit(solution)/shard_map/class_sums/pallas_call | solution.py:817
  61.5 0.0 collective-permute-done.9.high_after.refs_25_.refs_28_.refs_32_
  61.5 0.0 collective-permute-done.8.high_before.refs_24_.refs_27_.refs_31_
  61.5 0.0 collective-permute-done.7.low_after.refs_8_.refs_11_.refs_15_
  61.5 2.9 %collective-permute-done.6.low_before.refs_7_.refs_10_.refs_14_ = bf16[2880,128]{1,0:T(8,128)(2,1)} collective-permute-done((bf16[2880,128]{1,0:T(8,128)(2,1)}, bf16[2880,128]{1,0:T(8,128)(2,1)}, u32[]{:S(2)}, u32[]{:S(2)}) %collective-permute-start.6) | collective-permute-done | bytes 737312 | tf_op jit(solution)/shard_map/ppermute | solution.py:558
  64.4 2.2 %cut.1 = (bf16[1440,128]{1,0:T(8,128)(2,1)}, bf16[1440,128]{1,0:T(8,128)(2,1)}, bf16[1440,128]{1,0:T(8,128)(2,1)}, bf16[1440,128]{1,0:T(8,128)(2,1)}) custom-call(bf16[2880,128]{1,0:T(8,128)(2,1)} %collective-permute-done.6.low_before.refs_7_.refs_10_.refs_14_, bf16[2880,128]{1,0:T(8,128)(2,1)} %collective-permute-done.7.low_after.refs_8_.refs_11_.refs_15_, ...), custom_call_target="tpu_custom_call" | custom-call | flops 2000000000 | bytes 6000000 | tf_op jit(solution)/shard_map/cut/pallas_call | solution.py:620
  66.6 0.1 collective-permute-start.10
  66.7 2.7 %collective-permute-start.11 = (bf16[1440,128]{1,0:T(8,128)(2,1)}, bf16[1440,128]{1,0:T(8,128)(2,1)}, u32[]{:S(2)}, u32[]{:S(2)}) collective-permute-start(bf16[1440,128]{1,0:T(8,128)(2,1)} %get-tuple-element.30), channel_id=1, source_target_pairs={{0,3},{1,0},{2,1},{3,2},{4,7},{5,4},{6,5},{7,6},{8,11},{9,8},{10,9... | collective-permute-start | bytes 1105928 | tf_op jit(solution)/shard_map/ppermute | solution.py:558
  69.3 0.3 collective-permute-start.12
  69.7 1.1 %collective-permute-start.13 = (bf16[1440,128]{1,0:T(8,128)(2,1)}, bf16[1440,128]{1,0:T(8,128)(2,1)}, u32[]{:S(2)}, u32[]{:S(2)}) collective-permute-start(bf16[1440,128]{1,0:T(8,128)(2,1)} %get-tuple-element.32), channel_id=1, source_target_pairs={{0,12},{1,13},{2,14},{3,15},{4,0},{5,1},{6,2},{7,3},{8,4},{9,5},{1... | collective-permute-start | bytes 1105928 | tf_op jit(solution)/shard_map/ppermute | solution.py:558
  70.8 5.1 %all-to-all-start.1 = ((bf16[16,480,128]{2,1,0:T(8,128)(2,1)}), bf16[16,480,128]{2,1,0:T(8,128)(2,1)S(1)}, u32[]{:S(2)}, u32[]{:S(2)}) async-start(bf16[16,480,128]{2,1,0:T(8,128)(2,1)} %class_sums.1), calls=%async_computation.1 | async-start | bytes 3932160 | tf_op jit(solution)/shard_map/all_to_all | solution.py:904
  75.9 0.0 collective-permute-done.14
  75.9 0.1 collective-permute-done.10.refs_9_.refs_12_
  76.0 0.0 collective-permute-done.11.refs_13_.refs_16_
  76.1 1.0 collective-permute-done.12.refs_26_.refs_29_
  77.1 1.3 %collective-permute-done.13.refs_30_.refs_33_ = bf16[1440,128]{1,0:T(8,128)(2,1)} collective-permute-done((bf16[1440,128]{1,0:T(8,128)(2,1)}, bf16[1440,128]{1,0:T(8,128)(2,1)}, u32[]{:S(2)}, u32[]{:S(2)}) %collective-permute-start.13) | collective-permute-done | bytes 368672 | tf_op jit(solution)/shard_map/ppermute | solution.py:558
  78.3 9.6 %fold.1 = (bf16[18,48,512]{2,1,0:T(8,128)(2,1)}, bf16[18,48,512]{2,1,0:T(8,128)(2,1)}, f32[48,512]{1,0:T(8,128)}) custom-call(s32[1]{0:T(128)S(6)} %select_n.7.core, bf16[1920,128]{1,0:T(8,128)(2,1)} %harmonics.1.refs_0_.refs_17_, bf16[1920,128]{1,0:T(8,128)(2,1)} %collective-permute-done.left.refs_1_.refs_18_, ...), custom_call_target="tpu_custom_call" | custom-call | flops 8999999488 | bytes 27000000 | tf_op jit(solution)/shard_map/fold/pallas_call | solution.py:521
  87.9 14.1 %collective-permute-start.15 = (bf16[18,48,512]{2,1,0:T(8,128)(2,1)}, bf16[18,48,512]{2,1,0:T(8,128)(2,1)S(1)}, u32[]{:S(2)}, u32[]{:S(2)}) collective-permute-start(bf16[18,48,512]{2,1,0:T(8,128)(2,1)} %get-tuple-element.37), channel_id=1, source_target_pairs={{0,16},{16,0},{32,48},{48,32},{64,80},{80,64},{96,112},{112,96},{1... | collective-permute-start | bytes 2654216 | tf_op jit(solution)/shard_map/ppermute | solution.py:907
  101.9 2.3 %collective-permute-done.15.came = bf16[18,48,512]{2,1,0:T(8,128)(2,1)S(1)} collective-permute-done((bf16[18,48,512]{2,1,0:T(8,128)(2,1)}, bf16[18,48,512]{2,1,0:T(8,128)(2,1)S(1)}, u32[]{:S(2)}, u32[]{:S(2)}) %collective-permute-start.15) | collective-permute-done | bytes 884768 | tf_op jit(solution)/shard_map/ppermute | solution.py:907
  104.2 1.2 %copy-done.13 = bf16[18,48,512]{2,1,0:T(8,128)(2,1)S(1)} copy-done((bf16[18,48,512]{2,1,0:T(8,128)(2,1)S(1)}, bf16[18,48,512]{2,1,0:T(8,128)(2,1)}, u32[]{:S(2)}) %copy-start.13) | copy-done | bytes 884760
  105.4 0.9 copy-done.14
  106.3 2.6 %scores.1 = f32[1,48]{1,0:T(1,128)} custom-call(s32[1]{0:T(128)S(6)} %select_n.7.core, bf16[18,48,512]{2,1,0:T(8,128)(2,1)S(1)} %copy-done.13, bf16[18,48,512]{2,1,0:T(8,128)(2,1)S(1)} %collective-permute-done.15.came, f32[48,512]{1,0:T(8,128)S(1)} %copy-done.14), custom_call_target="tpu_custom_call" | custom-call | flops 3000000000 | bytes 9000000 | tf_op jit(solution)/shard_map/scores/pallas_call | solution.py:766
  108.9 0.0 all-to-all-done.1.arrived
  108.9 1.2 %averages.1 = f32[200,288]{1,0:T(8,128)} custom-call(s32[1]{0:T(128)} %bitcast.dom, bf16[16,480,128]{2,1,0:T(8,128)(2,1)S(1)} %all-to-all-done.1.arrived, f32[8,128,128]{2,1,0:T(8,128)S(1)} %copy-done.5), custom_call_target="tpu_custom_call" | custom-call | flops 2000000000 | bytes 6000000 | tf_op jit(solution)/shard_map/averages/pallas_call | solution.py:863
  (27 shorter events, 0.1 us)
Async XLA Ops:
  0.6 10.6 %copy-start.15 = (s32[48,2]{0,1:T(2,128)S(1)}, s32[48,2]{0,1:T(2,128)}, u32[]{:S(2)}) copy-start(s32[48,2]{0,1:T(2,128)} %param.24) | copy-start | bytes 1156
  0.7 10.6 %copy-start.16 = (s32[48]{0:T(128)S(1)}, s32[48]{0:T(128)}, u32[]{:S(2)}) copy-start(s32[48]{0:T(128)} %param.23) | copy-start | bytes 580
  0.7 10.6 %copy-start.17 = (s32[48,1]{0,1:T(1,128)S(1)}, s32[48,1]{0,1:T(1,128)}, u32[]{:S(2)}) copy-start(s32[48,1]{0,1:T(1,128)} %param.21) | copy-start | bytes 580
  0.7 10.6 %copy-start.18 = (s32[48]{0:T(128)S(1)}, s32[48]{0:T(128)}, u32[]{:S(2)}) copy-start(s32[48]{0:T(128)} %param.22) | copy-start | bytes 580
  0.7 10.6 %copy-start.19 = (s32[48]{0:T(128)S(1)}, s32[48]{0:T(128)}, u32[]{:S(2)}) copy-start(s32[48]{0:T(128)} %refs_37_.1) | copy-start | bytes 580
  0.7 18.5 %copy-start.4 = (f32[4,6,16,288]{3,2,1,0:T(8,128)S(1)}, f32[4,6,16,288]{3,2,1,0:T(8,128)}, u32[]{:S(2)}) copy-start(f32[4,6,16,288]{3,2,1,0:T(8,128)} %constant.49.clone.phases) | copy-start | bytes 1327108
  0.7 18.4 %copy-start.7 = (bf16[288,768]{1,0:T(8,128)(2,1)S(1)}, bf16[288,768]{1,0:T(8,128)(2,1)}, u32[]{:S(2)}) copy-start(bf16[288,768]{1,0:T(8,128)(2,1)} %constant.47.clone.wide) | copy-start | bytes 1327108
  0.7 18.4 %copy-start.8 = (bf16[288,288]{1,0:T(8,128)(2,1)S(1)}, bf16[288,288]{1,0:T(8,128)(2,1)}, u32[]{:S(2)}) copy-start(bf16[288,288]{1,0:T(8,128)(2,1)} %constant.48.clone.swap) | copy-start | bytes 497668
  0.7 18.4 %copy-start.10 = (f32[36,8,128]{2,1,0:T(8,128)S(1)}, f32[36,8,128]{2,1,0:T(8,128)}, u32[]{:S(2)}) copy-start(f32[36,8,128]{2,1,0:T(8,128)} %constant.50.clone.turn) | copy-start | bytes 442372
  0.7 18.4 %copy-start.11 = (f32[64,128]{1,0:T(8,128)S(1)}, f32[64,128]{1,0:T(8,128)}, u32[]{:S(2)}) copy-start(f32[64,128]{1,0:T(8,128)} %constant.51.clone.ctf_columns) | copy-start | bytes 98308
  4.9 14.0 %collective-permute-start.2 = (bf16[1920,128]{1,0:T(8,128)(2,1)}, bf16[1920,128]{1,0:T(8,128)(2,1)S(1)}, u32[]{:S(2)}, u32[]{:S(2)}) collective-permute-start(bf16[1920,128]{1,0:T(8,128)(2,1)} %harmonics.1.refs_0_.refs_17_), channel_id=1, source_target_pairs={{0,8},{1,9},{2,10},{3,11},{4,12},{5,13},{6,14},{7,15},{8,0},{9,1},... | collective-permute-start | bytes 1474568 | tf_op jit(solution)/shard_map/ppermute | solution.py:558
  6.1 30.9 %collective-permute-start.5 = (bf16[1920,128]{1,0:T(8,128)(2,1)}, bf16[1920,128]{1,0:T(8,128)(2,1)}, u32[]{:S(2)}, u32[]{:S(2)}) collective-permute-start(bf16[1920,128]{1,0:T(8,128)(2,1)} %harmonics.1.refs_0_.refs_17_), channel_id=1, source_target_pairs={{0,2},{1,3},{2,0},{3,1},{4,6},{5,7},{6,4},{7,5},{8,10},{9,11},{10,... | collective-permute-start | bytes 1474568 | tf_op jit(solution)/shard_map/ppermute | solution.py:558
  9.8 27.3 %collective-permute-start.4 = (bf16[1920,128]{1,0:T(8,128)(2,1)}, bf16[1920,128]{1,0:T(8,128)(2,1)}, u32[]{:S(2)}, u32[]{:S(2)}) collective-permute-start(bf16[1920,128]{1,0:T(8,128)(2,1)} %harmonics.1.refs_0_.refs_17_), channel_id=1, source_target_pairs={{0,3},{1,0},{2,1},{3,2},{4,7},{5,4},{6,5},{7,6},{8,11},{9,8},{10,9... | collective-permute-start | bytes 1474568 | tf_op jit(solution)/shard_map/ppermute | solution.py:558
  10.2 26.9 %collective-permute-start.3 = (bf16[1920,128]{1,0:T(8,128)(2,1)}, bf16[1920,128]{1,0:T(8,128)(2,1)}, u32[]{:S(2)}, u32[]{:S(2)}) collective-permute-start(bf16[1920,128]{1,0:T(8,128)(2,1)} %harmonics.1.refs_0_.refs_17_), channel_id=1, source_target_pairs={{0,1},{1,2},{2,3},{3,0},{4,5},{5,6},{6,7},{7,4},{8,9},{9,10},{10,1... | collective-permute-start | bytes 1474568 | tf_op jit(solution)/shard_map/ppermute | solution.py:558
  11.2 25.9 %collective-permute-start.1 = (bf16[1920,128]{1,0:T(8,128)(2,1)}, bf16[1920,128]{1,0:T(8,128)(2,1)}, u32[]{:S(2)}, u32[]{:S(2)}) collective-permute-start(bf16[1920,128]{1,0:T(8,128)(2,1)} %harmonics.1.refs_0_.refs_17_), channel_id=1, source_target_pairs={{0,12},{1,13},{2,14},{3,15},{4,0},{5,1},{6,2},{7,3},{8,4},{9,5},{1... | collective-permute-start | bytes 1474568 | tf_op jit(solution)/shard_map/ppermute | solution.py:558
  19.0 9.8 %copy-start.20 = (bf16[1920,128]{1,0:T(8,128)(2,1)}, bf16[1920,128]{1,0:T(8,128)(2,1)S(1)}, u32[]{:S(2)}) copy-start(bf16[1920,128]{1,0:T(8,128)(2,1)S(1)} %collective-permute-done.2.two_x.refs_3_.refs_20_) | copy-start | bytes 1474564
  19.0 18.1 %collective-permute-start = (bf16[1920,128]{1,0:T(8,128)(2,1)}, bf16[1920,128]{1,0:T(8,128)(2,1)}, u32[]{:S(2)}, u32[]{:S(2)}) collective-permute-start(bf16[1920,128]{1,0:T(8,128)(2,1)} %harmonics.1.refs_0_.refs_17_), channel_id=1, source_target_pairs={{0,4},{1,5},{2,6},{3,7},{4,8},{5,9},{6,10},{7,11},{8,12},{9,13},{1... | collective-permute-start | bytes 1474568 | tf_op jit(solution)/shard_map/ppermute | solution.py:558
  19.2 1.7 %copy-start.1 = (bf16[48,64,288]{2,1,0:T(8,128)(2,1)S(1)}, bf16[48,64,288]{2,1,0:T(8,128)(2,1)}, u32[]{:S(2)}) copy-start(bf16[48,64,288]{2,1,0:T(8,128)(2,1)} %param.19) | copy-start | bytes 5308420
  28.8 1.3 %copy-start = (bf16[7296,128]{1,0:T(8,128)(2,1)}, bf16[7296,128]{1,0:T(8,128)(2,1)S(1)}, u32[]{:S(2)}) copy-start(bf16[7296,128]{1,0:T(8,128)(2,1)S(1)} %spread.1) | copy-start | bytes 5603332
  30.0 28.5 %all-to-all-start = ((bf16[8,912,128]{2,1,0:T(8,128)(2,1)}), bf16[8,912,128]{2,1,0:T(8,128)(2,1)S(1)}, u32[]{:S(2)}, u32[]{:S(2)}) async-start(bf16[8,912,128]{2,1,0:T(8,128)(2,1)} %bitcast.16), calls=%async_computation | async-start | bytes 3735552 | tf_op jit(solution)/shard_map/all_to_all | solution.py:646
  37.1 9.0 %copy-start.2 = (bf16[48,64,288]{2,1,0:T(8,128)(2,1)S(1)}, bf16[48,64,288]{2,1,0:T(8,128)(2,1)}, u32[]{:S(2)}) copy-start(bf16[48,64,288]{2,1,0:T(8,128)(2,1)} %param.19) | copy-start | bytes 5308420
  37.1 9.0 %copy-start.9 = (bf16[288,288]{1,0:T(8,128)(2,1)S(1)}, bf16[288,288]{1,0:T(8,128)(2,1)}, u32[]{:S(2)}) copy-start(bf16[288,288]{1,0:T(8,128)(2,1)} %constant.48.clone.swap) | copy-start | bytes 497668
  37.1 9.0 %copy-start.12 = (f32[16,128]{1,0:T(8,128)S(1)}, f32[16,128]{1,0:T(8,128)}, u32[]{:S(2)}) copy-start(f32[16,128]{1,0:T(8,128)} %constant.52.clone.ctf_rows) | copy-start | bytes 24580
  39.6 21.9 %collective-permute-start.9 = (bf16[2880,128]{1,0:T(8,128)(2,1)}, bf16[2880,128]{1,0:T(8,128)(2,1)}, u32[]{:S(2)}, u32[]{:S(2)}) collective-permute-start(bf16[2880,128]{1,0:T(8,128)(2,1)} %get-tuple-element.23), channel_id=1, source_target_pairs={{0,12},{1,13},{2,14},{3,15},{4,0},{5,1},{6,2},{7,3},{8,4},{9,5},{1... | collective-permute-start | bytes 2211848 | tf_op jit(solution)/shard_map/ppermute | solution.py:558
  41.3 20.3 %collective-permute-start.8 = (bf16[2880,128]{1,0:T(8,128)(2,1)}, bf16[2880,128]{1,0:T(8,128)(2,1)}, u32[]{:S(2)}, u32[]{:S(2)}) collective-permute-start(bf16[2880,128]{1,0:T(8,128)(2,1)} %get-tuple-element.23), channel_id=1, source_target_pairs={{0,4},{1,5},{2,6},{3,7},{4,8},{5,9},{6,10},{7,11},{8,12},{9,13},{1... | collective-permute-start | bytes 2211848 | tf_op jit(solution)/shard_map/ppermute | solution.py:558
  42.3 19.2 %collective-permute-start.7 = (bf16[2880,128]{1,0:T(8,128)(2,1)}, bf16[2880,128]{1,0:T(8,128)(2,1)}, u32[]{:S(2)}, u32[]{:S(2)}) collective-permute-start(bf16[2880,128]{1,0:T(8,128)(2,1)} %get-tuple-element.22), channel_id=1, source_target_pairs={{0,3},{1,0},{2,1},{3,2},{4,7},{5,4},{6,5},{7,6},{8,11},{9,8},{10,9... | collective-permute-start | bytes 2211848 | tf_op jit(solution)/shard_map/ppermute | solution.py:558
  46.1 18.3 %collective-permute-start.6 = (bf16[2880,128]{1,0:T(8,128)(2,1)}, bf16[2880,128]{1,0:T(8,128)(2,1)}, u32[]{:S(2)}, u32[]{:S(2)}) collective-permute-start(bf16[2880,128]{1,0:T(8,128)(2,1)} %get-tuple-element.22), channel_id=1, source_target_pairs={{0,1},{1,2},{2,3},{3,0},{4,5},{5,6},{6,7},{7,4},{8,9},{9,10},{10,1... | collective-permute-start | bytes 2211848 | tf_op jit(solution)/shard_map/ppermute | solution.py:558
  46.1 1.0 copy-start.6
  54.5 0.9 copy-start.3
  55.4 20.5 %collective-permute-start.14 = (bf16[3456,128]{1,0:T(8,128)(2,1)S(1)}, bf16[3456,128]{1,0:T(8,128)(2,1)}, u32[]{:S(2)}, u32[]{:S(2)}) collective-permute-start(bf16[3456,128]{1,0:T(8,128)(2,1)S(1)} %get-tuple-element.35), channel_id=1, source_target_pairs={{0,16},{16,0},{32,48},{48,32},{64,80},{80,64},{96,112},{112,96},{1... | collective-permute-start | bytes 2654216 | tf_op jit(solution)/shard_map/ppermute | solution.py:903
  66.6 9.4 %collective-permute-start.10 = (bf16[1440,128]{1,0:T(8,128)(2,1)}, bf16[1440,128]{1,0:T(8,128)(2,1)S(1)}, u32[]{:S(2)}, u32[]{:S(2)}) collective-permute-start(bf16[1440,128]{1,0:T(8,128)(2,1)} %get-tuple-element.29), channel_id=1, source_target_pairs={{0,1},{1,2},{2,3},{3,0},{4,5},{5,6},{6,7},{7,4},{8,9},{9,10},{10,1... | collective-permute-start | bytes 1105928 | tf_op jit(solution)/shard_map/ppermute | solution.py:558
  66.7 9.4 %collective-permute-start.11 = (bf16[1440,128]{1,0:T(8,128)(2,1)}, bf16[1440,128]{1,0:T(8,128)(2,1)}, u32[]{:S(2)}, u32[]{:S(2)}) collective-permute-start(bf16[1440,128]{1,0:T(8,128)(2,1)} %get-tuple-element.30), channel_id=1, source_target_pairs={{0,3},{1,0},{2,1},{3,2},{4,7},{5,4},{6,5},{7,6},{8,11},{9,8},{10,9... | collective-permute-start | bytes 1105928 | tf_op jit(solution)/shard_map/ppermute | solution.py:558
  69.3 7.7 %collective-permute-start.12 = (bf16[1440,128]{1,0:T(8,128)(2,1)}, bf16[1440,128]{1,0:T(8,128)(2,1)}, u32[]{:S(2)}, u32[]{:S(2)}) collective-permute-start(bf16[1440,128]{1,0:T(8,128)(2,1)} %get-tuple-element.31), channel_id=1, source_target_pairs={{0,4},{1,5},{2,6},{3,7},{4,8},{5,9},{6,10},{7,11},{8,12},{9,13},{1... | collective-permute-start | bytes 1105928 | tf_op jit(solution)/shard_map/ppermute | solution.py:558
  69.7 8.6 %collective-permute-start.13 = (bf16[1440,128]{1,0:T(8,128)(2,1)}, bf16[1440,128]{1,0:T(8,128)(2,1)}, u32[]{:S(2)}, u32[]{:S(2)}) collective-permute-start(bf16[1440,128]{1,0:T(8,128)(2,1)} %get-tuple-element.32), channel_id=1, source_target_pairs={{0,12},{1,13},{2,14},{3,15},{4,0},{5,1},{6,2},{7,3},{8,4},{9,5},{1... | collective-permute-start | bytes 1105928 | tf_op jit(solution)/shard_map/ppermute | solution.py:558
  70.8 38.1 %all-to-all-start.1 = ((bf16[16,480,128]{2,1,0:T(8,128)(2,1)}), bf16[16,480,128]{2,1,0:T(8,128)(2,1)S(1)}, u32[]{:S(2)}, u32[]{:S(2)}) async-start(bf16[16,480,128]{2,1,0:T(8,128)(2,1)} %class_sums.1), calls=%async_computation.1 | async-start | bytes 3932160 | tf_op jit(solution)/shard_map/all_to_all | solution.py:904
  76.0 2.3 %copy-start.21 = (bf16[1440,128]{1,0:T(8,128)(2,1)}, bf16[1440,128]{1,0:T(8,128)(2,1)S(1)}, u32[]{:S(2)}) copy-start(bf16[1440,128]{1,0:T(8,128)(2,1)S(1)} %collective-permute-done.10.refs_9_.refs_12_) | copy-start | bytes 1105924
  87.9 16.3 %collective-permute-start.15 = (bf16[18,48,512]{2,1,0:T(8,128)(2,1)}, bf16[18,48,512]{2,1,0:T(8,128)(2,1)S(1)}, u32[]{:S(2)}, u32[]{:S(2)}) collective-permute-start(bf16[18,48,512]{2,1,0:T(8,128)(2,1)} %get-tuple-element.37), channel_id=1, source_target_pairs={{0,16},{16,0},{32,48},{48,32},{64,80},{80,64},{96,112},{112,96},{1... | collective-permute-start | bytes 2654216 | tf_op jit(solution)/shard_map/ppermute | solution.py:907
  104.2 1.2 %copy-start.13 = (bf16[18,48,512]{2,1,0:T(8,128)(2,1)S(1)}, bf16[18,48,512]{2,1,0:T(8,128)(2,1)}, u32[]{:S(2)}) copy-start(bf16[18,48,512]{2,1,0:T(8,128)(2,1)} %get-tuple-element.36.kept) | copy-start | bytes 2654212
  105.4 0.9 copy-start.14
  106.3 2.6 %copy-start.5 = (f32[8,128,128]{2,1,0:T(8,128)S(1)}, f32[8,128,128]{2,1,0:T(8,128)}, u32[]{:S(2)}) copy-start(f32[8,128,128]{2,1,0:T(8,128)} %constant.53.clone.squares) | copy-start | bytes 1572868

commit v2 on v1

--- a/solution.py
+++ b/solution.py
@@ -905,6 +905,7 @@
     class_average = averages(dom, sums).reshape(KD, BAND, ROW)
     kept, sent, norm = fold(core, gathered, own, far, defocus)
     came = lax.ppermute(sent, "dom", swap)
+    came, class_average = lax.optimization_barrier((came, class_average))
     best_score = scores(core, kept, came, norm).reshape(PD)
     return (best_score, class_average)
 

time: 111 us -> 111 us (level)
  the two profiles are of different devices: /device:TPU:23 before, /device:TPU:0 now
where the time goes in v2:
time: 111 us
  Pallas kernels  40.5 us (36%)
  starting transfers between devices  35 us (32%)
  waiting for transfers between devices  28.9 us (26%)
  local copies, waits for them, and re-layouts  5.02 us (5%)
    ppermute x14, starting transfers between devices, moved_by(): return lax.ppermute(value, 'cls', moves)  26.2 us
    ppermute x14, waiting for transfers between devices, moved_by(): return lax.ppermute(value, 'cls', moves)  15 us
    pallas_call x1, Pallas kernels, fold(): pl.pallas_call(functools.partial(fold_kernel, layout, count), in_specs=[p...  9.6 us
    pallas_call x1, Pallas kernels, spread_bands(): pl.pallas_call(spread_kernel, grid_spec=pltpu.PrefetchScalarGridSpec(num_...  7.99 us
    pallas_call x1, Pallas kernels, weighted_spectra(): pl.pallas_call(weight_kernel, grid_spec=pltpu.PrefetchScalarGridSpec(num_...  7.34 us
    all_to_all x1, waiting for transfers between devices, on_device(): sums = lax.all_to_all(sums, 'cls', 0, 0, tiled=True)  7.19 us
    all_to_all x1, waiting for transfers between devices, gather_blocks(): lax.all_to_all(spread.reshape(DOM, UROWS, 128), 'dom', 0, 0, tiled=True)  6.74 us
    unnamed x44, local copies, waits for them, and re-layouts  4.99 us
  transfers between devices with their start and end apart: 18, of which 8 were waited for; matrix products, arithmetic and copies ran while one was open for 0% of the time, Pallas kernels for 31%

profile of v2, /device:TPU:0, one launch (start us, length us, event | category | flops | bytes accessed | tf_op | source)
XLA Modules:
  0.0 110.5 jit_solution(7748259125475817269)
XLA Ops:
  0.6 0.0 copy-start.15
  0.7 0.0 copy-start.19
  0.7 0.0 copy-start.4
  0.7 0.0 copy-start.7
  0.7 0.0 copy-start.8
  0.7 0.0 copy-start.10
  0.7 0.0 copy-start.11
  0.8 4.2 %harmonics.1.refs_0_.refs_17_ = bf16[1920,128]{1,0:T(8,128)(2,1)} custom-call(s32[1]{0:T(128)S(6)} %select_n.7.core, bf16[1600,288]{1,0:T(8,128)(2,1)} %bitcast.24, bf16[2,320,288]{2,1,0:T(8,128)(2,1)} %constant.45.clone.table_any.table, f32[2,128,128]{2,1,0:T(8,128)} %constant.46.clone.squares_any), custom_call_target="tpu_custom_call" | custom-call | flops 4000000000 | bytes 12000000 | tf_op jit(solution)/shard_map/harmonics/pallas_call | solution.py:210
  4.9 3.2 %collective-permute-start.2 = (bf16[1920,128]{1,0:T(8,128)(2,1)}, bf16[1920,128]{1,0:T(8,128)(2,1)S(1)}, u32[]{:S(2)}, u32[]{:S(2)}) collective-permute-start(bf16[1920,128]{1,0:T(8,128)(2,1)} %harmonics.1.refs_0_.refs_17_), channel_id=1, source_target_pairs={{0,8},{1,9},{2,10},{3,11},{4,12},{5,13},{6,14},{7,15},{8,0},{9,1},... | collective-permute-start | bytes 1474568 | tf_op jit(solution)/shard_map/ppermute | solution.py:558
  8.1 3.9 %collective-permute-start.5 = (bf16[1920,128]{1,0:T(8,128)(2,1)}, bf16[1920,128]{1,0:T(8,128)(2,1)}, u32[]{:S(2)}, u32[]{:S(2)}) collective-permute-start(bf16[1920,128]{1,0:T(8,128)(2,1)} %harmonics.1.refs_0_.refs_17_), channel_id=1, source_target_pairs={{0,2},{1,3},{2,0},{3,1},{4,6},{5,7},{6,4},{7,5},{8,10},{9,11},{10,... | collective-permute-start | bytes 1474568 | tf_op jit(solution)/shard_map/ppermute | solution.py:558
  12.0 0.7 collective-permute-start.4
  12.7 1.3 %collective-permute-start.3 = (bf16[1920,128]{1,0:T(8,128)(2,1)}, bf16[1920,128]{1,0:T(8,128)(2,1)}, u32[]{:S(2)}, u32[]{:S(2)}) collective-permute-start(bf16[1920,128]{1,0:T(8,128)(2,1)} %harmonics.1.refs_0_.refs_17_), channel_id=1, source_target_pairs={{0,1},{1,2},{2,3},{3,0},{4,5},{5,6},{6,7},{7,4},{8,9},{9,10},{10,1... | collective-permute-start | bytes 1474568 | tf_op jit(solution)/shard_map/ppermute | solution.py:558
  14.0 1.1 %collective-permute-start.1 = (bf16[1920,128]{1,0:T(8,128)(2,1)}, bf16[1920,128]{1,0:T(8,128)(2,1)}, u32[]{:S(2)}, u32[]{:S(2)}) collective-permute-start(bf16[1920,128]{1,0:T(8,128)(2,1)} %harmonics.1.refs_0_.refs_17_), channel_id=1, source_target_pairs={{0,12},{1,13},{2,14},{3,15},{4,0},{5,1},{6,2},{7,3},{8,4},{9,5},{1... | collective-permute-start | bytes 1474568 | tf_op jit(solution)/shard_map/ppermute | solution.py:558
  15.2 4.3 %collective-permute-done.2.two_x.refs_3_.refs_20_ = bf16[1920,128]{1,0:T(8,128)(2,1)S(1)} collective-permute-done((bf16[1920,128]{1,0:T(8,128)(2,1)}, bf16[1920,128]{1,0:T(8,128)(2,1)S(1)}, u32[]{:S(2)}, u32[]{:S(2)}) %collective-permute-start.2) | collective-permute-done | bytes 491552 | tf_op jit(solution)/shard_map/ppermute | solution.py:558
  19.6 2.9 %collective-permute-start = (bf16[1920,128]{1,0:T(8,128)(2,1)}, bf16[1920,128]{1,0:T(8,128)(2,1)}, u32[]{:S(2)}, u32[]{:S(2)}) collective-permute-start(bf16[1920,128]{1,0:T(8,128)(2,1)} %harmonics.1.refs_0_.refs_17_), channel_id=1, source_target_pairs={{0,4},{1,5},{2,6},{3,7},{4,8},{5,9},{6,10},{7,11},{8,12},{9,13},{1... | collective-permute-start | bytes 1474568 | tf_op jit(solution)/shard_map/ppermute | solution.py:558
  22.5 0.0 copy-done.7
  22.5 0.0 copy-start.1
  22.5 1.7 %copy-done.1 = bf16[48,64,288]{2,1,0:T(8,128)(2,1)S(1)} copy-done((bf16[48,64,288]{2,1,0:T(8,128)(2,1)S(1)}, bf16[48,64,288]{2,1,0:T(8,128)(2,1)}, u32[]{:S(2)}) %copy-start.1) | copy-done | bytes 1769496
  24.2 8.0 %spread.1 = bf16[7296,128]{1,0:T(8,128)(2,1)S(1)} custom-call(s32[6,48]{1,0:T(8,128)S(1)} %stack.15.scalars, bf16[3072,288]{1,0:T(8,128)(2,1)S(1)} %bitcast.17, bf16[288,768]{1,0:T(8,128)(2,1)S(1)} %copy-done.7, bf16[288,288]{1,0:T(8,128)(2,1)S(1)} %copy-done.8, f32[4,6,16,288]{3,2,1,0:T(8,128)S(1)} %copy-done.4, f32[36,8,128]{2,1,0:T(8,128)S(1)} %copy-done.10, ...), custom_call_target="tpu_custom_call" | custom-call | flops 8999999488 | bytes 27000000 | tf_op jit(solution)/shard_map/spread/pallas_call | solution.py:321
  32.2 1.3 %copy-done = bf16[7296,128]{1,0:T(8,128)(2,1)} copy-done((bf16[7296,128]{1,0:T(8,128)(2,1)}, bf16[7296,128]{1,0:T(8,128)(2,1)S(1)}, u32[]{:S(2)}) %copy-start) | copy-done | bytes 1867800
  33.5 4.5 %all-to-all-start = ((bf16[8,912,128]{2,1,0:T(8,128)(2,1)}), bf16[8,912,128]{2,1,0:T(8,128)(2,1)S(1)}, u32[]{:S(2)}, u32[]{:S(2)}) async-start(bf16[8,912,128]{2,1,0:T(8,128)(2,1)} %bitcast.16), calls=%async_computation | async-start | bytes 3735552 | tf_op jit(solution)/shard_map/all_to_all | solution.py:646
  37.9 0.0 copy-start.9
  38.0 0.0 copy-start.12
  38.0 0.0 collective-permute-done.5.two_z.refs_6_.refs_23_
  38.0 0.0 collective-permute-done.4.up.refs_5_.refs_22_
  38.0 0.0 collective-permute-done.3.down.refs_4_.refs_21_
  38.0 0.0 collective-permute-done.1.right.refs_2_.refs_19_
  38.0 0.0 collective-permute-done.left.refs_1_.refs_18_
  38.0 2.5 %join.1 = (bf16[2880,128]{1,0:T(8,128)(2,1)}, bf16[2880,128]{1,0:T(8,128)(2,1)}) custom-call(bf16[1920,128]{1,0:T(8,128)(2,1)} %collective-permute-done.left.refs_1_.refs_18_, bf16[1920,128]{1,0:T(8,128)(2,1)} %collective-permute-done.1.right.refs_2_.refs_19_, bf16[1920,128]{1,0:T(8,128)(2,1)} %copy-done.20, ...), custom_call_target="tpu_custom_call" | custom-call | flops 2000000000 | bytes 6000000 | tf_op jit(solution)/shard_map/join/pallas_call | solution.py:583
  40.5 1.5 %collective-permute-start.9 = (bf16[2880,128]{1,0:T(8,128)(2,1)}, bf16[2880,128]{1,0:T(8,128)(2,1)}, u32[]{:S(2)}, u32[]{:S(2)}) collective-permute-start(bf16[2880,128]{1,0:T(8,128)(2,1)} %get-tuple-element.25), channel_id=1, source_target_pairs={{0,12},{1,13},{2,14},{3,15},{4,0},{5,1},{6,2},{7,3},{8,4},{9,5},{1... | collective-permute-start | bytes 2211848 | tf_op jit(solution)/shard_map/ppermute | solution.py:558
  42.0 0.6 collective-permute-start.8
  42.6 4.0 %collective-permute-start.7 = (bf16[2880,128]{1,0:T(8,128)(2,1)}, bf16[2880,128]{1,0:T(8,128)(2,1)}, u32[]{:S(2)}, u32[]{:S(2)}) collective-permute-start(bf16[2880,128]{1,0:T(8,128)(2,1)} %get-tuple-element.24), channel_id=1, source_target_pairs={{0,3},{1,0},{2,1},{3,2},{4,7},{5,4},{6,5},{7,6},{8,11},{9,8},{10,9... | collective-permute-start | bytes 2211848 | tf_op jit(solution)/shard_map/ppermute | solution.py:558
  46.6 0.0 collective-permute-start.6
  46.6 0.0 copy-done.12
  46.6 0.0 copy-start.6
  46.6 1.0 copy-done.6
  47.7 7.3 %weights.1 = (bf16[3456,128]{1,0:T(8,128)(2,1)S(1)}, bf16[3456,128]{1,0:T(8,128)(2,1)S(1)}) custom-call(s32[1]{0:T(128)S(6)} %select_n.7.core, s32[6,48]{1,0:T(8,128)S(1)} %stack.15.scalars, bf16[3072,288]{1,0:T(8,128)(2,1)S(1)} %bitcast.18, bf16[2,320,288]{2,1,0:T(8,128)(2,1)S(1)} %copy-done.6, bf16[288,288]{1,0:T(8,128)(2,1)S(1)} %copy-done.9, ...), custom_call_target="tpu_custom_call" | custom-call | flops 10000000000 | bytes 30000000 | tf_op jit(solution)/shard_map/weights/pallas_call | solution.py:395
  55.0 0.9 copy-done.3
  55.9 0.0 collective-permute-start.14
  55.9 6.7 %all-to-all-done.arrived = bf16[8,912,128]{2,1,0:T(8,128)(2,1)S(1)} async-done(((bf16[8,912,128]{2,1,0:T(8,128)(2,1)}), bf16[8,912,128]{2,1,0:T(8,128)(2,1)S(1)}, u32[]{:S(2)}, u32[]{:S(2)}) %all-to-all-start) | async-done | bytes 1867808 | tf_op jit(solution)/shard_map/all_to_all | solution.py:646
  62.7 3.0 %class_sums.1 = bf16[16,480,128]{2,1,0:T(8,128)(2,1)} custom-call(bf16[8,912,128]{2,1,0:T(8,128)(2,1)S(1)} %all-to-all-done.arrived), custom_call_target="tpu_custom_call" | custom-call | flops 3000000000 | bytes 9000000 | tf_op jit(solution)/shard_map/class_sums/pallas_call | solution.py:817
  65.7 0.0 collective-permute-done.9.high_after.refs_25_.refs_28_.refs_32_
  65.7 0.0 collective-permute-done.8.high_before.refs_24_.refs_27_.refs_31_
  65.7 0.0 collective-permute-done.7.low_after.refs_8_.refs_11_.refs_15_
  65.7 0.5 collective-permute-done.6.low_before.refs_7_.refs_10_.refs_14_
  66.2 2.2 %cut.1 = (bf16[1440,128]{1,0:T(8,128)(2,1)}, bf16[1440,128]{1,0:T(8,128)(2,1)}, bf16[1440,128]{1,0:T(8,128)(2,1)}, bf16[1440,128]{1,0:T(8,128)(2,1)}) custom-call(bf16[2880,128]{1,0:T(8,128)(2,1)} %collective-permute-done.6.low_before.refs_7_.refs_10_.refs_14_, bf16[2880,128]{1,0:T(8,128)(2,1)} %collective-permute-done.7.low_after.refs_8_.refs_11_.refs_15_, ...), custom_call_target="tpu_custom_call" | custom-call | flops 2000000000 | bytes 6000000 | tf_op jit(solution)/shard_map/cut/pallas_call | solution.py:620
  68.4 1.5 %collective-permute-start.10 = (bf16[1440,128]{1,0:T(8,128)(2,1)}, bf16[1440,128]{1,0:T(8,128)(2,1)S(1)}, u32[]{:S(2)}, u32[]{:S(2)}) collective-permute-start(bf16[1440,128]{1,0:T(8,128)(2,1)} %get-tuple-element.31), channel_id=1, source_target_pairs={{0,1},{1,2},{2,3},{3,0},{4,5},{5,6},{6,7},{7,4},{8,9},{9,10},{10,1... | collective-permute-start | bytes 1105928 | tf_op jit(solution)/shard_map/ppermute | solution.py:558
  69.9 2.2 %collective-permute-start.11 = (bf16[1440,128]{1,0:T(8,128)(2,1)}, bf16[1440,128]{1,0:T(8,128)(2,1)}, u32[]{:S(2)}, u32[]{:S(2)}) collective-permute-start(bf16[1440,128]{1,0:T(8,128)(2,1)} %get-tuple-element.32), channel_id=1, source_target_pairs={{0,3},{1,0},{2,1},{3,2},{4,7},{5,4},{6,5},{7,6},{8,11},{9,8},{10,9... | collective-permute-start | bytes 1105928 | tf_op jit(solution)/shard_map/ppermute | solution.py:558
  72.1 0.6 collective-permute-start.12
  72.7 2.6 %collective-permute-start.13 = (bf16[1440,128]{1,0:T(8,128)(2,1)}, bf16[1440,128]{1,0:T(8,128)(2,1)}, u32[]{:S(2)}, u32[]{:S(2)}) collective-permute-start(bf16[1440,128]{1,0:T(8,128)(2,1)} %get-tuple-element.34), channel_id=1, source_target_pairs={{0,12},{1,13},{2,14},{3,15},{4,0},{5,1},{6,2},{7,3},{8,4},{9,5},{1... | collective-permute-start | bytes 1105928 | tf_op jit(solution)/shard_map/ppermute | solution.py:558
  75.3 4.3 %all-to-all-start.1 = ((bf16[16,480,128]{2,1,0:T(8,128)(2,1)}), bf16[16,480,128]{2,1,0:T(8,128)(2,1)S(1)}, u32[]{:S(2)}, u32[]{:S(2)}) async-start(bf16[16,480,128]{2,1,0:T(8,128)(2,1)} %class_sums.1), calls=%async_computation.1 | async-start | bytes 3932160 | tf_op jit(solution)/shard_map/all_to_all | solution.py:904
  79.6 0.0 collective-permute-done.14
  79.6 1.0 collective-permute-done.10.refs_9_.refs_12_
  80.6 2.0 %collective-permute-done.11.refs_13_.refs_16_ = bf16[1440,128]{1,0:T(8,128)(2,1)} collective-permute-done((bf16[1440,128]{1,0:T(8,128)(2,1)}, bf16[1440,128]{1,0:T(8,128)(2,1)}, u32[]{:S(2)}, u32[]{:S(2)}) %collective-permute-start.11) | collective-permute-done | bytes 368672 | tf_op jit(solution)/shard_map/ppermute | solution.py:558
  82.6 2.4 %collective-permute-done.12.refs_26_.refs_29_ = bf16[1440,128]{1,0:T(8,128)(2,1)} collective-permute-done((bf16[1440,128]{1,0:T(8,128)(2,1)}, bf16[1440,128]{1,0:T(8,128)(2,1)}, u32[]{:S(2)}, u32[]{:S(2)}) %collective-permute-start.12) | collective-permute-done | bytes 368672 | tf_op jit(solution)/shard_map/ppermute | solution.py:558
  85.0 4.8 %collective-permute-done.13.refs_30_.refs_33_ = bf16[1440,128]{1,0:T(8,128)(2,1)} collective-permute-done((bf16[1440,128]{1,0:T(8,128)(2,1)}, bf16[1440,128]{1,0:T(8,128)(2,1)}, u32[]{:S(2)}, u32[]{:S(2)}) %collective-permute-start.13) | collective-permute-done | bytes 368672 | tf_op jit(solution)/shard_map/ppermute | solution.py:558
  89.8 9.6 %fold.1 = (bf16[18,48,512]{2,1,0:T(8,128)(2,1)}, bf16[18,48,512]{2,1,0:T(8,128)(2,1)}, f32[48,512]{1,0:T(8,128)}) custom-call(s32[1]{0:T(128)S(6)} %select_n.7.core, bf16[1920,128]{1,0:T(8,128)(2,1)} %harmonics.1.refs_0_.refs_17_, bf16[1920,128]{1,0:T(8,128)(2,1)} %collective-permute-done.left.refs_1_.refs_18_, ...), custom_call_target="tpu_custom_call" | custom-call | flops 8999999488 | bytes 27000000 | tf_op jit(solution)/shard_map/fold/pallas_call | solution.py:521
  99.4 0.0 copy-start.14
  99.4 0.1 collective-permute-start.15
  99.5 7.2 %all-to-all-done.1.arrived = bf16[16,480,128]{2,1,0:T(8,128)(2,1)S(1)} async-done(((bf16[16,480,128]{2,1,0:T(8,128)(2,1)}), bf16[16,480,128]{2,1,0:T(8,128)(2,1)S(1)}, u32[]{:S(2)}, u32[]{:S(2)}) %all-to-all-start.1) | async-done | bytes 1966112 | tf_op jit(solution)/shard_map/all_to_all | solution.py:904
  106.7 1.2 %averages.1 = f32[200,288]{1,0:T(8,128)} custom-call(s32[1]{0:T(128)} %bitcast.dom, bf16[16,480,128]{2,1,0:T(8,128)(2,1)S(1)} %all-to-all-done.1.arrived, f32[8,128,128]{2,1,0:T(8,128)S(1)} %copy-done.5), custom_call_target="tpu_custom_call" | custom-call | flops 2000000000 | bytes 6000000 | tf_op jit(solution)/shard_map/averages/pallas_call | solution.py:863
  107.9 0.0 collective-permute-done.15.came
  107.9 0.0 copy-done.13
  107.9 2.6 %scores.1 = f32[1,48]{1,0:T(1,128)} custom-call(s32[1]{0:T(128)S(6)} %select_n.7.core, bf16[18,48,512]{2,1,0:T(8,128)(2,1)S(1)} %copy-done.13, bf16[18,48,512]{2,1,0:T(8,128)(2,1)S(1)} %collective-permute-done.15.came, f32[48,512]{1,0:T(8,128)S(1)} %copy-done.14), custom_call_target="tpu_custom_call" | custom-call | flops 3000000000 | bytes 9000000 | tf_op jit(solution)/shard_map/scores/pallas_call | solution.py:766
  (27 shorter events, 0.1 us)
Async XLA Ops:
  0.6 14.5 %copy-start.15 = (s32[48,2]{0,1:T(2,128)S(1)}, s32[48,2]{0,1:T(2,128)}, u32[]{:S(2)}) copy-start(s32[48,2]{0,1:T(2,128)} %param.24) | copy-start | bytes 1156
  0.7 14.5 %copy-start.16 = (s32[48]{0:T(128)S(1)}, s32[48]{0:T(128)}, u32[]{:S(2)}) copy-start(s32[48]{0:T(128)} %param.23) | copy-start | bytes 580
  0.7 14.5 %copy-start.17 = (s32[48,1]{0,1:T(1,128)S(1)}, s32[48,1]{0,1:T(1,128)}, u32[]{:S(2)}) copy-start(s32[48,1]{0,1:T(1,128)} %param.21) | copy-start | bytes 580
  0.7 14.5 %copy-start.18 = (s32[48]{0:T(128)S(1)}, s32[48]{0:T(128)}, u32[]{:S(2)}) copy-start(s32[48]{0:T(128)} %param.22) | copy-start | bytes 580
  0.7 14.5 %copy-start.19 = (s32[48]{0:T(128)S(1)}, s32[48]{0:T(128)}, u32[]{:S(2)}) copy-start(s32[48]{0:T(128)} %refs_37_.1) | copy-start | bytes 580
  0.7 21.8 %copy-start.4 = (f32[4,6,16,288]{3,2,1,0:T(8,128)S(1)}, f32[4,6,16,288]{3,2,1,0:T(8,128)}, u32[]{:S(2)}) copy-start(f32[4,6,16,288]{3,2,1,0:T(8,128)} %constant.49.clone.phases) | copy-start | bytes 1327108
  0.7 21.8 %copy-start.7 = (bf16[288,768]{1,0:T(8,128)(2,1)S(1)}, bf16[288,768]{1,0:T(8,128)(2,1)}, u32[]{:S(2)}) copy-start(bf16[288,768]{1,0:T(8,128)(2,1)} %constant.47.clone.wide) | copy-start | bytes 1327108
  0.7 21.8 %copy-start.8 = (bf16[288,288]{1,0:T(8,128)(2,1)S(1)}, bf16[288,288]{1,0:T(8,128)(2,1)}, u32[]{:S(2)}) copy-start(bf16[288,288]{1,0:T(8,128)(2,1)} %constant.48.clone.swap) | copy-start | bytes 497668
  0.7 21.7 %copy-start.10 = (f32[36,8,128]{2,1,0:T(8,128)S(1)}, f32[36,8,128]{2,1,0:T(8,128)}, u32[]{:S(2)}) copy-start(f32[36,8,128]{2,1,0:T(8,128)} %constant.50.clone.turn) | copy-start | bytes 442372
  0.7 21.7 %copy-start.11 = (f32[64,128]{1,0:T(8,128)S(1)}, f32[64,128]{1,0:T(8,128)}, u32[]{:S(2)}) copy-start(f32[64,128]{1,0:T(8,128)} %constant.51.clone.ctf_columns) | copy-start | bytes 98308
  4.9 14.6 %collective-permute-start.2 = (bf16[1920,128]{1,0:T(8,128)(2,1)}, bf16[1920,128]{1,0:T(8,128)(2,1)S(1)}, u32[]{:S(2)}, u32[]{:S(2)}) collective-permute-start(bf16[1920,128]{1,0:T(8,128)(2,1)} %harmonics.1.refs_0_.refs_17_), channel_id=1, source_target_pairs={{0,8},{1,9},{2,10},{3,11},{4,12},{5,13},{6,14},{7,15},{8,0},{9,1},... | collective-permute-start | bytes 1474568 | tf_op jit(solution)/shard_map/ppermute | solution.py:558
  8.1 29.8 %collective-permute-start.5 = (bf16[1920,128]{1,0:T(8,128)(2,1)}, bf16[1920,128]{1,0:T(8,128)(2,1)}, u32[]{:S(2)}, u32[]{:S(2)}) collective-permute-start(bf16[1920,128]{1,0:T(8,128)(2,1)} %harmonics.1.refs_0_.refs_17_), channel_id=1, source_target_pairs={{0,2},{1,3},{2,0},{3,1},{4,6},{5,7},{6,4},{7,5},{8,10},{9,11},{10,... | collective-permute-start | bytes 1474568 | tf_op jit(solution)/shard_map/ppermute | solution.py:558
  12.0 26.0 %collective-permute-start.4 = (bf16[1920,128]{1,0:T(8,128)(2,1)}, bf16[1920,128]{1,0:T(8,128)(2,1)}, u32[]{:S(2)}, u32[]{:S(2)}) collective-permute-start(bf16[1920,128]{1,0:T(8,128)(2,1)} %harmonics.1.refs_0_.refs_17_), channel_id=1, source_target_pairs={{0,3},{1,0},{2,1},{3,2},{4,7},{5,4},{6,5},{7,6},{8,11},{9,8},{10,9... | collective-permute-start | bytes 1474568 | tf_op jit(solution)/shard_map/ppermute | solution.py:558
  12.7 25.3 %collective-permute-start.3 = (bf16[1920,128]{1,0:T(8,128)(2,1)}, bf16[1920,128]{1,0:T(8,128)(2,1)}, u32[]{:S(2)}, u32[]{:S(2)}) collective-permute-start(bf16[1920,128]{1,0:T(8,128)(2,1)} %harmonics.1.refs_0_.refs_17_), channel_id=1, source_target_pairs={{0,1},{1,2},{2,3},{3,0},{4,5},{5,6},{6,7},{7,4},{8,9},{9,10},{10,1... | collective-permute-start | bytes 1474568 | tf_op jit(solution)/shard_map/ppermute | solution.py:558
  14.0 24.0 %collective-permute-start.1 = (bf16[1920,128]{1,0:T(8,128)(2,1)}, bf16[1920,128]{1,0:T(8,128)(2,1)}, u32[]{:S(2)}, u32[]{:S(2)}) collective-permute-start(bf16[1920,128]{1,0:T(8,128)(2,1)} %harmonics.1.refs_0_.refs_17_), channel_id=1, source_target_pairs={{0,12},{1,13},{2,14},{3,15},{4,0},{5,1},{6,2},{7,3},{8,4},{9,5},{1... | collective-permute-start | bytes 1474568 | tf_op jit(solution)/shard_map/ppermute | solution.py:558
  19.6 12.6 %copy-start.20 = (bf16[1920,128]{1,0:T(8,128)(2,1)}, bf16[1920,128]{1,0:T(8,128)(2,1)S(1)}, u32[]{:S(2)}) copy-start(bf16[1920,128]{1,0:T(8,128)(2,1)S(1)} %collective-permute-done.2.two_x.refs_3_.refs_20_) | copy-start | bytes 1474564
  19.6 18.5 %collective-permute-start = (bf16[1920,128]{1,0:T(8,128)(2,1)}, bf16[1920,128]{1,0:T(8,128)(2,1)}, u32[]{:S(2)}, u32[]{:S(2)}) collective-permute-start(bf16[1920,128]{1,0:T(8,128)(2,1)} %harmonics.1.refs_0_.refs_17_), channel_id=1, source_target_pairs={{0,4},{1,5},{2,6},{3,7},{4,8},{5,9},{6,10},{7,11},{8,12},{9,13},{1... | collective-permute-start | bytes 1474568 | tf_op jit(solution)/shard_map/ppermute | solution.py:558
  22.5 1.7 %copy-start.1 = (bf16[48,64,288]{2,1,0:T(8,128)(2,1)S(1)}, bf16[48,64,288]{2,1,0:T(8,128)(2,1)}, u32[]{:S(2)}) copy-start(bf16[48,64,288]{2,1,0:T(8,128)(2,1)} %param.19) | copy-start | bytes 5308420
  32.2 1.3 %copy-start = (bf16[7296,128]{1,0:T(8,128)(2,1)}, bf16[7296,128]{1,0:T(8,128)(2,1)S(1)}, u32[]{:S(2)}) copy-start(bf16[7296,128]{1,0:T(8,128)(2,1)S(1)} %spread.1) | copy-start | bytes 5603332
  33.5 29.2 %all-to-all-start = ((bf16[8,912,128]{2,1,0:T(8,128)(2,1)}), bf16[8,912,128]{2,1,0:T(8,128)(2,1)S(1)}, u32[]{:S(2)}, u32[]{:S(2)}) async-start(bf16[8,912,128]{2,1,0:T(8,128)(2,1)} %bitcast.16), calls=%async_computation | async-start | bytes 3735552 | tf_op jit(solution)/shard_map/all_to_all | solution.py:646
  37.9 8.7 %copy-start.2 = (bf16[48,64,288]{2,1,0:T(8,128)(2,1)S(1)}, bf16[48,64,288]{2,1,0:T(8,128)(2,1)}, u32[]{:S(2)}) copy-start(bf16[48,64,288]{2,1,0:T(8,128)(2,1)} %param.19) | copy-start | bytes 5308420
  37.9 8.7 %copy-start.9 = (bf16[288,288]{1,0:T(8,128)(2,1)S(1)}, bf16[288,288]{1,0:T(8,128)(2,1)}, u32[]{:S(2)}) copy-start(bf16[288,288]{1,0:T(8,128)(2,1)} %constant.48.clone.swap) | copy-start | bytes 497668
  38.0 8.7 %copy-start.12 = (f32[16,128]{1,0:T(8,128)S(1)}, f32[16,128]{1,0:T(8,128)}, u32[]{:S(2)}) copy-start(f32[16,128]{1,0:T(8,128)} %constant.52.clone.ctf_rows) | copy-start | bytes 24580
  40.5 25.2 %collective-permute-start.9 = (bf16[2880,128]{1,0:T(8,128)(2,1)}, bf16[2880,128]{1,0:T(8,128)(2,1)}, u32[]{:S(2)}, u32[]{:S(2)}) collective-permute-start(bf16[2880,128]{1,0:T(8,128)(2,1)} %get-tuple-element.25), channel_id=1, source_target_pairs={{0,12},{1,13},{2,14},{3,15},{4,0},{5,1},{6,2},{7,3},{8,4},{9,5},{1... | collective-permute-start | bytes 2211848 | tf_op jit(solution)/shard_map/ppermute | solution.py:558
  42.0 23.7 %collective-permute-start.8 = (bf16[2880,128]{1,0:T(8,128)(2,1)}, bf16[2880,128]{1,0:T(8,128)(2,1)}, u32[]{:S(2)}, u32[]{:S(2)}) collective-permute-start(bf16[2880,128]{1,0:T(8,128)(2,1)} %get-tuple-element.25), channel_id=1, source_target_pairs={{0,4},{1,5},{2,6},{3,7},{4,8},{5,9},{6,10},{7,11},{8,12},{9,13},{1... | collective-permute-start | bytes 2211848 | tf_op jit(solution)/shard_map/ppermute | solution.py:558
  42.6 23.1 %collective-permute-start.7 = (bf16[2880,128]{1,0:T(8,128)(2,1)}, bf16[2880,128]{1,0:T(8,128)(2,1)}, u32[]{:S(2)}, u32[]{:S(2)}) collective-permute-start(bf16[2880,128]{1,0:T(8,128)(2,1)} %get-tuple-element.24), channel_id=1, source_target_pairs={{0,3},{1,0},{2,1},{3,2},{4,7},{5,4},{6,5},{7,6},{8,11},{9,8},{10,9... | collective-permute-start | bytes 2211848 | tf_op jit(solution)/shard_map/ppermute | solution.py:558
  46.6 19.6 %collective-permute-start.6 = (bf16[2880,128]{1,0:T(8,128)(2,1)}, bf16[2880,128]{1,0:T(8,128)(2,1)}, u32[]{:S(2)}, u32[]{:S(2)}) collective-permute-start(bf16[2880,128]{1,0:T(8,128)(2,1)} %get-tuple-element.24), channel_id=1, source_target_pairs={{0,1},{1,2},{2,3},{3,0},{4,5},{5,6},{6,7},{7,4},{8,9},{9,10},{10,1... | collective-permute-start | bytes 2211848 | tf_op jit(solution)/shard_map/ppermute | solution.py:558
  46.6 1.0 copy-start.6
  55.0 0.9 copy-start.3
  55.9 23.6 %collective-permute-start.14 = (bf16[3456,128]{1,0:T(8,128)(2,1)S(1)}, bf16[3456,128]{1,0:T(8,128)(2,1)}, u32[]{:S(2)}, u32[]{:S(2)}) collective-permute-start(bf16[3456,128]{1,0:T(8,128)(2,1)S(1)} %get-tuple-element.37), channel_id=1, source_target_pairs={{0,16},{16,0},{32,48},{48,32},{64,80},{80,64},{96,112},{112,96},{1... | collective-permute-start | bytes 2654216 | tf_op jit(solution)/shard_map/ppermute | solution.py:903
  68.4 12.2 %collective-permute-start.10 = (bf16[1440,128]{1,0:T(8,128)(2,1)}, bf16[1440,128]{1,0:T(8,128)(2,1)S(1)}, u32[]{:S(2)}, u32[]{:S(2)}) collective-permute-start(bf16[1440,128]{1,0:T(8,128)(2,1)} %get-tuple-element.31), channel_id=1, source_target_pairs={{0,1},{1,2},{2,3},{3,0},{4,5},{5,6},{6,7},{7,4},{8,9},{9,10},{10,1... | collective-permute-start | bytes 1105928 | tf_op jit(solution)/shard_map/ppermute | solution.py:558
  69.9 12.7 %collective-permute-start.11 = (bf16[1440,128]{1,0:T(8,128)(2,1)}, bf16[1440,128]{1,0:T(8,128)(2,1)}, u32[]{:S(2)}, u32[]{:S(2)}) collective-permute-start(bf16[1440,128]{1,0:T(8,128)(2,1)} %get-tuple-element.32), channel_id=1, source_target_pairs={{0,3},{1,0},{2,1},{3,2},{4,7},{5,4},{6,5},{7,6},{8,11},{9,8},{10,9... | collective-permute-start | bytes 1105928 | tf_op jit(solution)/shard_map/ppermute | solution.py:558
  72.1 12.9 %collective-permute-start.12 = (bf16[1440,128]{1,0:T(8,128)(2,1)}, bf16[1440,128]{1,0:T(8,128)(2,1)}, u32[]{:S(2)}, u32[]{:S(2)}) collective-permute-start(bf16[1440,128]{1,0:T(8,128)(2,1)} %get-tuple-element.33), channel_id=1, source_target_pairs={{0,4},{1,5},{2,6},{3,7},{4,8},{5,9},{6,10},{7,11},{8,12},{9,13},{1... | collective-permute-start | bytes 1105928 | tf_op jit(solution)/shard_map/ppermute | solution.py:558
  72.7 17.1 %collective-permute-start.13 = (bf16[1440,128]{1,0:T(8,128)(2,1)}, bf16[1440,128]{1,0:T(8,128)(2,1)}, u32[]{:S(2)}, u32[]{:S(2)}) collective-permute-start(bf16[1440,128]{1,0:T(8,128)(2,1)} %get-tuple-element.34), channel_id=1, source_target_pairs={{0,12},{1,13},{2,14},{3,15},{4,0},{5,1},{6,2},{7,3},{8,4},{9,5},{1... | collective-permute-start | bytes 1105928 | tf_op jit(solution)/shard_map/ppermute | solution.py:558
  75.3 31.4 %all-to-all-start.1 = ((bf16[16,480,128]{2,1,0:T(8,128)(2,1)}), bf16[16,480,128]{2,1,0:T(8,128)(2,1)S(1)}, u32[]{:S(2)}, u32[]{:S(2)}) async-start(bf16[16,480,128]{2,1,0:T(8,128)(2,1)} %class_sums.1), calls=%async_computation.1 | async-start | bytes 3932160 | tf_op jit(solution)/shard_map/all_to_all | solution.py:904
  80.6 9.2 %copy-start.21 = (bf16[1440,128]{1,0:T(8,128)(2,1)}, bf16[1440,128]{1,0:T(8,128)(2,1)S(1)}, u32[]{:S(2)}) copy-start(bf16[1440,128]{1,0:T(8,128)(2,1)S(1)} %collective-permute-done.10.refs_9_.refs_12_) | copy-start | bytes 1105924
  89.8 16.9 %copy-start.5 = (f32[8,128,128]{2,1,0:T(8,128)S(1)}, f32[8,128,128]{2,1,0:T(8,128)}, u32[]{:S(2)}) copy-start(f32[8,128,128]{2,1,0:T(8,128)} %constant.53.clone.squares) | copy-start | bytes 1572868
  99.4 8.5 %copy-start.14 = (f32[48,512]{1,0:T(8,128)S(1)}, f32[48,512]{1,0:T(8,128)}, u32[]{:S(2)}) copy-start(f32[48,512]{1,0:T(8,128)} %get-tuple-element.42.norm) | copy-start | bytes 294916
  99.4 8.5 %collective-permute-start.15 = (bf16[18,48,512]{2,1,0:T(8,128)(2,1)}, bf16[18,48,512]{2,1,0:T(8,128)(2,1)S(1)}, u32[]{:S(2)}, u32[]{:S(2)}) collective-permute-start(bf16[18,48,512]{2,1,0:T(8,128)(2,1)} %get-tuple-element.39), channel_id=1, source_target_pairs={{0,16},{16,0},{32,48},{48,32},{64,80},{80,64},{96,112},{112,96},{1... | collective-permute-start | bytes 2654216 | tf_op jit(solution)/shard_map/ppermute | solution.py:907
  106.7 1.2 %copy-start.13 = (bf16[18,48,512]{2,1,0:T(8,128)(2,1)S(1)}, bf16[18,48,512]{2,1,0:T(8,128)(2,1)}, u32[]{:S(2)}) copy-start(bf16[18,48,512]{2,1,0:T(8,128)(2,1)} %get-tuple-element.38.kept) | copy-start | bytes 2654212
